TPU v7x, 128 devices: a whole 4x4x4 slice. The times are simulated.
128 devices in a mesh: dp: 4 (over z), expert: 32 (over x, y, core).
Axes of the slice: x: 4, y: 4, z: 4, core: 2. Of those that a mesh axis runs over, the one named last changes fastest.
Arguments:
- hidden: bfloat16 [12288, 2880], P('expert', 'dp'), may hold values from -6 to 6
- segments: int32 [32, 384], P('expert'), may hold values from 0 to 3, never falling along the last dimension, each value on 1 to 192 neighbouring positions
- request_adapter: int32 [32, 4], P('expert'), may hold values from 0 to 7
- routes: int32 [32, 384, 4], P('expert', 'dp'), may hold values from 0 to 31, all different within a row; in each aligned block of 96 rows (0 to 95, 96 to 191, ..., all dimensions but the last counted through in order) at most 16 rows name the same one
- expert_gates: bfloat16 [32, 384, 4], P('expert', 'dp'), may hold values from 0.049804688 to 0.59765625
- attention_gain: float32 [2880], replicated, may hold values from 0.25 to 1.75
- joined_weight: bfloat16 [2880, 4, 640], P(None, 'dp'), may hold values from -0.109375 to 0.109375
- sinks: float32 [32], P('dp'), may hold values from 0 to 3
- attention_out_weight: bfloat16 [2048, 2880], P('dp'), may hold values from -0.125 to 0.125
- joined_down_maps: bfloat16 [2880, 128], replicated, may hold values from -0.109375 to 0.109375
- joined_up_maps: bfloat16 [128, 4, 640], P(None, 'dp'), may hold values from -0.375 to 0.375
- output_down_maps: bfloat16 [2048, 128], P('dp'), may hold values from -0.125 to 0.125
- output_up_maps: bfloat16 [128, 2880], P(None, 'dp'), may hold values from -0.75 to 0.75
- expert_norm_gain: float32 [2880], replicated, may hold values from 0.25 to 1.75
- expert_gate_weight: bfloat16 [32, 2880, 2880], P('expert', None, 'dp'), may hold values from -0.109375 to 0.109375
- expert_up_weight: bfloat16 [32, 2880, 2880], P('expert', None, 'dp'), may hold values from -0.109375 to 0.109375
- expert_down_weight: bfloat16 [32, 2880, 2880], P('expert', 'dp'), may hold values from -0.109375 to 0.109375
- closing_gain: float32 [2880], replicated, may hold values from 0.25 to 1.75
- vocabulary_weight: bfloat16 [2880, 102400], P(None, ('dp', 'expert')), may hold values from -0.109375 to 0.109375
Outputs:
- hidden_out: bfloat16 [12288, 2880], P('expert', 'dp')
- logits: float32 [128, 102400], P(None, ('dp', 'expert'))
Inputs may be any that keep to these rules, and one draw needn't show every extreme that they name: `segments`: in each column the ids do not fall; each of the 4 requests has 1 to 192 tokens, and one has exactly 192. `routes`: the 4 experts of a token differ. Within the rows of one device (96 consecutive tokens, aligned blocks) no expert is named more than 16 times, and in some blocks one expert is named exactly 16 times.
All inputs are finite; a program needn't handle non-finite values.
Results may differ from a plain program's by a relative error of at most 0.02.
Values may be sent and summed in bfloat16 or wider, within the bound.
A program may use at most 128 MiB of HBM per device.

v0:
```python
import jax
import jax.numpy as jnp
from jax import lax
from jax.sharding import PartitionSpec as P

HEAD_SIZE = 64
QUERY_GROUP = 8
TOP = 4
ADAPTER_RANK = 16
REQS = 4


epsilon = 1e-05
theta_base = 150000.0
adapter_scale = 2.0
glu_alpha = 1.702


def rms_scale(values, gain_row):
    mean_square = jnp.mean(values * values, axis=-1, keepdims=True)
    return values * lax.rsqrt(mean_square + epsilon) * gain_row


def positions_of(segment_row):
    counter = jnp.arange(segment_row.shape[0], dtype=jnp.int32)
    starting = jnp.concatenate(
        [jnp.ones((1,), dtype=jnp.bool_), segment_row[1:] != segment_row[:-1]]
    )
    first_index = lax.cummax(jnp.where(starting, counter, 0), axis=0)
    return counter - first_index


def adapter_per_token(segment_row, adapter_row):
    hits = segment_row[:, None] == jnp.arange(adapter_row.shape[0], dtype=jnp.int32)[None, :]
    return jnp.sum(jnp.where(hits, adapter_row[None, :], 0), axis=1)


def rotate_heads(values, positions):
    head_dim = values.shape[-1]
    half_dim = head_dim // 2
    frequency = theta_base ** (-2.0 * jnp.arange(half_dim, dtype=jnp.float32) / head_dim)
    angles = positions.astype(jnp.float32)[:, None] * frequency[None, :]
    cosine = jnp.cos(angles)[:, None, :]
    sine_part = jnp.sin(angles)[:, None, :]
    first_half = values[..., :half_dim]
    second_half = values[..., half_dim:]
    return jnp.concatenate(
        [
            first_half * cosine - second_half * sine_part,
            second_half * cosine + first_half * sine_part,
        ],
        axis=-1,
    )


def attend_heads(queries, key_heads, value_heads, segment_row, sink_row):
    tokens_now, kv_now, group_now, head_dim = queries.shape
    scores = jnp.einsum(
        "tkgh,skh->kgts", queries, key_heads, preferred_element_type=jnp.float32
    ) * head_dim ** (-0.5)
    counter = jnp.arange(tokens_now, dtype=jnp.int32)
    allowed = (segment_row[:, None] == segment_row[None, :]) & (
        counter[None, :] <= counter[:, None]
    )
    weights = jnp.where(allowed[None, None], jnp.exp(scores), 0.0)
    totals = jnp.sum(weights, axis=-1, keepdims=True) + jnp.exp(sink_row).reshape(
        kv_now, group_now, 1, 1
    )
    probs = (weights / totals).astype(jnp.bfloat16)
    blended_hidden = jnp.einsum(
        "kgts,skh->tkgh", probs, value_heads, preferred_element_type=jnp.float32
    )
    return blended_hidden.astype(jnp.bfloat16).reshape(tokens_now, kv_now * group_now * head_dim)


def shards(
    hidden,
    segments,
    request_adapter,
    routes,
    expert_gates,
    attention_gain,
    joined_weight,
    sinks,
    attention_out_weight,
    joined_down_maps,
    joined_up_maps,
    output_down_maps,
    output_up_maps,
    expert_norm_gain,
    expert_gate_weight,
    expert_up_weight,
    expert_down_weight,
    closing_gain,
    vocabulary_weight,
):
    groups = lax.axis_size("dp")
    columns = lax.axis_size("expert")
    position_dp = lax.axis_index("dp")
    segment_row = segments[0]
    adapter_row = request_adapter[0]
    col_tokens = segment_row.shape[0]
    gathered_rows = lax.all_gather(hidden, "dp", axis=1, tiled=True)
    width = gathered_rows.shape[1]
    normalized_hidden = rms_scale(gathered_rows.astype(jnp.float32), attention_gain).astype(
        jnp.bfloat16
    )
    joined_projection = jnp.dot(
        normalized_hidden, joined_weight.reshape(width, -1), preferred_element_type=jnp.float32
    )
    reduced_every_adapter = joined_down_maps.shape[1]
    reduced_hidden = jnp.dot(
        normalized_hidden, joined_down_maps, preferred_element_type=jnp.float32
    ).astype(jnp.bfloat16)
    rank_owner = jnp.arange(reduced_every_adapter, dtype=jnp.int32) // ADAPTER_RANK
    adapter_mask = adapter_per_token(segment_row, adapter_row)[:, None] == rank_owner[None, :]
    selected_reduced = jnp.where(adapter_mask, reduced_hidden, jnp.zeros_like(reduced_hidden))
    joined_projection = joined_projection + adapter_scale * jnp.dot(
        selected_reduced,
        joined_up_maps.reshape(reduced_every_adapter, -1),
        preferred_element_type=jnp.float32,
    )
    kv_here = joined_weight.shape[1]
    joined_projection = joined_projection.reshape(col_tokens, kv_here, QUERY_GROUP + 2, HEAD_SIZE)
    positions = positions_of(segment_row)
    queries = rotate_heads(
        joined_projection[:, :, :QUERY_GROUP].reshape(col_tokens, kv_here * QUERY_GROUP, HEAD_SIZE),
        positions,
    )
    queries = queries.astype(jnp.bfloat16).reshape(col_tokens, kv_here, QUERY_GROUP, HEAD_SIZE)
    key_heads = rotate_heads(joined_projection[:, :, QUERY_GROUP], positions).astype(jnp.bfloat16)
    value_heads = joined_projection[:, :, QUERY_GROUP + 1].astype(jnp.bfloat16)
    blended_hidden = attend_heads(queries, key_heads, value_heads, segment_row, sinks)
    partial_out = jnp.dot(blended_hidden, attention_out_weight, preferred_element_type=jnp.float32)
    mine_out = lax.psum_scatter(
        partial_out.astype(jnp.bfloat16), "dp", scatter_dimension=1, tiled=True
    ).astype(jnp.float32)
    output_reduced = lax.psum(
        jnp.dot(blended_hidden, output_down_maps, preferred_element_type=jnp.float32).astype(
            jnp.bfloat16
        ),
        "dp",
    )
    selected_output = jnp.where(adapter_mask, output_reduced, jnp.zeros_like(output_reduced))
    adapter_delta = adapter_scale * jnp.dot(
        selected_output, output_up_maps, preferred_element_type=jnp.float32
    )
    resid = (hidden.astype(jnp.float32) + mine_out + adapter_delta).astype(jnp.bfloat16)
    share = col_tokens // groups
    column_full = lax.all_gather(resid, "dp", axis=1, tiled=True)
    own_rows = lax.dynamic_slice_in_dim(column_full, position_dp * share, share, 0)
    moe_in = rms_scale(
        lax.optimization_barrier(own_rows).astype(jnp.float32), expert_norm_gain
    ).astype(jnp.bfloat16)
    experts = expert_gate_weight.shape[0] * columns
    capacity = 4 * share * TOP // (3 * experts)
    route_flat = routes[0].reshape(-1)
    one_hot = (route_flat[:, None] == jnp.arange(experts, dtype=jnp.int32)[None, :]).astype(
        jnp.int32
    )
    slot_rows = jnp.sum((jnp.cumsum(one_hot, axis=0) - one_hot) * one_hot, axis=1)
    target = route_flat * capacity + slot_rows
    source_rows = jnp.arange(route_flat.shape[0], dtype=jnp.int32) // TOP
    table = jnp.full((experts * capacity,), share, jnp.int32).at[target].set(source_rows)
    padded = jnp.concatenate([moe_in, jnp.zeros((1, width), jnp.bfloat16)], axis=0)
    outgoing = jnp.take(padded, table, axis=0).reshape(experts, capacity, width)
    gate_weight = expert_gate_weight[0]
    up_weight = expert_up_weight[0]
    down_weight = expert_down_weight[0]
    copies = jnp.tile(outgoing, (groups, 1, 1))
    arrived = lax.all_to_all(copies, ("dp", "expert"), split_axis=0, concat_axis=0, tiled=True)
    senders = arrived.shape[0]
    slots_now = arrived.shape[1]
    rows_in = arrived.reshape(-1, width)
    gate_part = jnp.dot(rows_in, gate_weight, preferred_element_type=jnp.float32)
    up_part = jnp.dot(rows_in, up_weight, preferred_element_type=jnp.float32)
    activated = (gate_part * jax.nn.sigmoid(glu_alpha * gate_part) * (up_part + 1.0)).astype(
        jnp.bfloat16
    )
    shares_out = (
        jnp.dot(activated, down_weight, preferred_element_type=jnp.float32)
        .astype(jnp.bfloat16)
        .reshape(senders, slots_now, width)
    )
    answers = lax.all_to_all(shares_out, ("dp", "expert"), split_axis=0, concat_axis=0, tiled=True)
    merged = jnp.sum(
        answers.reshape(groups, columns, capacity, width).astype(jnp.float32), axis=0
    ).astype(jnp.bfloat16)
    picked_out = jnp.take(merged.reshape(experts * capacity, width), target, axis=0).reshape(
        share, TOP, width
    )
    mixture = jnp.einsum(
        "tk,tkd->td", expert_gates[0], picked_out, preferred_element_type=jnp.float32
    )
    moe_rounded = lax.optimization_barrier(mixture.astype(jnp.bfloat16))
    finished = (own_rows.astype(jnp.float32) + moe_rounded.astype(jnp.float32)).astype(jnp.bfloat16)
    hidden_out = lax.all_to_all(finished, "dp", split_axis=1, concat_axis=0, tiled=True)
    counter = jnp.arange(col_tokens, dtype=jnp.int32)
    request_ids = jnp.arange(REQS, dtype=jnp.int32)
    last_index = jnp.max(
        jnp.where(segment_row[None, :] == request_ids[:, None], counter[None, :], -1), axis=1
    )
    local_index = last_index - position_dp * share
    inside = (local_index >= 0) & (local_index < share)
    chosen = jnp.take(finished, jnp.clip(local_index, 0, share - 1), axis=0)
    chosen = jnp.where(inside[:, None], chosen, jnp.zeros_like(chosen))
    ends = rms_scale(chosen.astype(jnp.float32), closing_gain).astype(jnp.bfloat16)
    spread_rows = lax.all_gather(ends, ("dp", "expert"), axis=0, tiled=True)
    tail_rows = jnp.sum(
        spread_rows.reshape(groups, columns * REQS, width).astype(jnp.float32), axis=0
    ).astype(jnp.bfloat16)
    logits = jnp.dot(tail_rows, vocabulary_weight, preferred_element_type=jnp.float32)
    return (hidden_out, logits)


def solution(mesh):
    in_specs = (
        P("expert", "dp"),
        P("expert", None),
        P("expert", None),
        P("expert", "dp", None),
        P("expert", "dp", None),
        P(),
        P(None, "dp", None),
        P("dp"),
        P("dp", None),
        P(),
        P(None, "dp", None),
        P("dp", None),
        P(None, "dp"),
        P(),
        P("expert", None, "dp"),
        P("expert", None, "dp"),
        P("expert", "dp", None),
        P(),
        P(None, ("dp", "expert")),
    )
    out_specs = (P("expert", "dp"), P(None, ("dp", "expert")))
    return jax.shard_map(shards, mesh=mesh, in_specs=in_specs, out_specs=out_specs, check_vma=False)
```

profile of v0, /device:TPU:1, one launch (start us, length us, event | category | flops | bytes accessed | tf_op | source)
XLA Modules:
  0.0 658.6 jit_solution(9227070420197901265)
XLA Ops:
  12.1 32.8 %all-gather.5.cloned.1.call-done = bf16[384,2880]{0,1:T(8,128)(2,1)} async-done(((bf16[384,720]{0,1:T(8,128)(2,1)}), bf16[384,2880]{0,1:T(8,128)(2,1)}) %all-gather.5.cloned.1.call-update) | async-done | bytes 2211856 | tf_op jit(solution)/shard_map/all_gather | solution.py:103
  44.9 2.2 fusion
  47.1 5.9 fusion.11
  53.1 4.8 fusion.21
  57.9 2.5 copy.62
  64.2 2.2 fusion.23
  68.2 4.1 convolution_convert_fusion.1
  72.5 35.0 %all-reduce.3.cloned.1.call-done = bf16[384,128]{1,0:T(8,128)(2,1)} async-done(((bf16[384,128]{1,0:T(8,128)(2,1)}), bf16[384,128]{1,0:T(8,128)(2,1)}) %all-reduce.3.cloned.1.call-update) | async-done | bytes 98320 | tf_op jit(solution)/shard_map/psum | solution.py:138
  107.5 35.9 %reduce-scatter.2.cloned.1.call-done = bf16[384,720]{0,1:T(8,128)(2,1)} async-done(((bf16[384,2880]{0,1:T(8,128)(2,1)}), bf16[384,720]{0,1:T(8,128)(2,1)}) %reduce-scatter.2.cloned.1.call-update) | async-done | bytes 552976 | tf_op jit(solution)/shard_map/reduce_scatter | solution.py:135
  143.4 2.4 fusion.22
  147.7 3.2 scatter_custom_fusion
  151.0 26.5 %all-gather.7.cloned.1.call-done = bf16[384,2880]{0,1:T(8,128)(2,1)} async-done(((bf16[384,720]{0,1:T(8,128)(2,1)}), bf16[384,2880]{0,1:T(8,128)(2,1)}) %all-gather.7.cloned.1.call-update) | async-done | bytes 2211856 | tf_op jit(solution)/shard_map/all_gather | solution.py:150
  180.4 3.7 gather_fusion
  184.1 2.2 broadcast_select_fusion
  186.4 5.2 tile.8
  191.6 145.7 %all_to_all.29 = bf16[128,16,2880]{2,1,0:T(8,128)(2,1)} all-to-all(bf16[128,16,2880]{2,1,0:T(8,128)(2,1)} %bitcast.126), channel_id=1, replica_groups=mesh['dp'=4,'expert'=32] {'dp','expert'}, dimensions={0} | all-to-all | bytes 23592960 | tf_op jit(solution)/shard_map/all_to_all | solution.py:171
  337.3 15.1 %fusion.4 = f32[2048,720]{0,1:T(8,128)} fusion(bf16[2048,2880]{1,0:T(8,128)(2,1)} %bitcast.25, bf16[1,2880,720]{1,2,0:T(8,128)(2,1)} %param.34), kind=kOutput, calls=%fused_computation.15 | convolution fusion | flops 8493465600 | bytes 21841920 | tf_op jit(solution)/shard_map/dot_general | solution.py:176
  352.4 26.6 %convolution_convert_fusion = bf16[2048,2880]{0,1:T(8,128)(2,1)} fusion(bf16[1,720,2880]{2,1,0:T(8,128)(2,1)} %param.35, f32[2048,720]{0,1:T(8,128)} %fusion.4, bf16[2048,2880]{1,0:T(8,128)(2,1)} %bitcast.25, bf16[1,2880,720]{1,2,0:T(8,128)(2,1)} %param.33), kind=kOutput, calls=%fused_computation.4 | convolution fusion | flops 17004625920 | bytes 37785600 | tf_op jit(solution)/shard_map/dot_general | solution.py:181
  379.0 16.3 %copy.71 = bf16[2048,2880]{1,0:T(8,128)(2,1)} copy(bf16[2048,2880]{0,1:T(8,128)(2,1)} %convolution_convert_fusion) | data formatting | bytes 23592960 | tf_op jit(solution)/shard_map/convert_element_type | solution.py:182
  395.4 5.6 all-to-all-start.1
  401.0 9.6 %all-gather.9.cloned.1.call-start = ((), (), s32[]{:S(2)}) async-start(), calls=%async_computation.8 | async-start | bytes 3038208 | tf_op jit(solution)/shard_map/all_gather | solution.py:208
  411.2 134.0 %all-to-all-done.1 = bf16[128,16,2880]{2,1,0:T(8,128)(2,1)} async-done(((bf16[128,16,2880]{2,1,0:T(8,128)(2,1)}), bf16[128,16,2880]{2,1,0:T(8,128)(2,1)}, u32[]{:S(2)}, u32[]{:S(2)}) %all-to-all-start.1) | async-done | bytes 11796512 | tf_op jit(solution)/shard_map/all_to_all | solution.py:185
  545.2 8.1 %reduce_sum.89 = bf16[32,16,2880]{2,1,0:T(8,128)(2,1)S(1)} reduce(bf16[4,32,16,2880]{3,2,1,0:T(8,128)(2,1)} %bitcast.30, bf16[]{:T(256)} %constant.119.clone.1), dimensions={0}, to_apply=%region_12.13 | reduce | flops 4423680 | bytes 14745602 | tf_op jit(solution)/shard_map/reduce_sum | solution.py:186
  553.3 3.5 gather_fusion.1
  556.8 2.6 gather.19
  559.4 4.7 multiply_reduce_fusion
  564.4 1.7 add_convert_fusion
  568.3 11.6 %all_to_all.30 = bf16[96,4,720]{2,0,1:T(8,128)(2,1)S(1)} all-to-all(bf16[96,4,720]{2,0,1:T(8,128)(2,1)S(1)} %copy.72), channel_id=1, replica_groups=mesh['dp'=4,'expert'=32] {'dp'}, dimensions={1} | all-to-all | bytes 1105920 | tf_op jit(solution)/shard_map/all_to_all | solution.py:197
  580.9 57.2 %all-gather.9.cloned.1.call-done = bf16[128,4,2880]{2,1,0:T(4,128)(2,1)} async-done(((bf16[1,4,2880]{2,1,0:T(4,128)(2,1)}), bf16[128,4,2880]{2,1,0:T(4,128)(2,1)}) %all-gather.9.cloned.1.call-update) | async-done | bytes 2949136 | tf_op jit(solution)/shard_map/all_gather | solution.py:208
  638.1 5.8 reshape.444
  643.8 3.4 reduce_sum.91
  647.2 4.7 fusion.80
  (95 shorter events, 19.5 us)
Async XLA Ops:
  7.2 61.1 %copy-start = (bf16[512,2880]{0,1:T(8,128)(2,1)S(1)}, bf16[512,2880]{0,1:T(8,128)(2,1)}, u32[]{:S(2)}) copy-start(bf16[512,2880]{0,1:T(8,128)(2,1)} %param.27) | copy-start | bytes 8847364
  7.2 37.8 %all-gather.5.cloned.1.call-start = ((), (), s32[]{:S(2)}) async-start(), calls=%async_computation.4 | async-start | bytes 2764800 | tf_op jit(solution)/shard_map/all_gather | solution.py:103
  7.9 99.6 %all-reduce.3.cloned.1.call-start = ((), (), s32[]{:S(2)}) async-start(), calls=%async_computation.6 | async-start | bytes 196608 | tf_op jit(solution)/shard_map/psum | solution.py:138
  47.1 6.0 copy-start.9
  47.1 6.0 copy-start.10
  64.2 3.0 copy-start.4
  66.4 0.8 copy-start.3
  68.2 75.2 %copy-start.2 = (bf16[384,720]{0,1:T(8,128)(2,1)S(1)}, bf16[384,720]{0,1:T(8,128)(2,1)}, u32[]{:S(2)}) copy-start(bf16[384,720]{0,1:T(8,128)(2,1)} %param.19) | copy-start | bytes 1658884
  68.2 75.2 %reduce-scatter.2.cloned.1.call-start = ((), (), s32[]{:S(2)}) async-start(), calls=%async_computation.5 | async-start | bytes 2764800 | tf_op jit(solution)/shard_map/reduce_scatter | solution.py:135
  72.4 73.5 %copy-start.5 = (s32[1,96,4]{1,2,0:T(4,128)S(1)}, s32[1,96,4]{1,2,0:T(4,128)}, u32[]{:S(2)}) copy-start(s32[1,96,4]{1,2,0:T(4,128)} %param.22) | copy-start | bytes 4612
  72.4 107.2 %copy-start.6 = (f32[2880]{0:T(1024)S(1)}, f32[2880]{0:T(1024)}, u32[]{:S(2)}) copy-start(f32[2880]{0:T(1024)} %param.32) | copy-start | bytes 34564
  72.4 105.1 %all-gather.7.cloned.1.call-start = ((), (), s32[]{:S(2)}) async-start(), calls=%async_computation.7 | async-start | bytes 2764800 | tf_op jit(solution)/shard_map/all_gather | solution.py:150
  395.4 15.6 %copy-start.8 = (bf16[1,96,4]{1,2,0:T(4,128)(2,1)S(1)}, bf16[1,96,4]{1,2,0:T(4,128)(2,1)}, u32[]{:S(2)}) copy-start(bf16[1,96,4]{1,2,0:T(4,128)(2,1)} %param.23) | copy-start | bytes 2308
  395.4 149.8 %all-to-all-start.1 = ((bf16[128,16,2880]{2,1,0:T(8,128)(2,1)}), bf16[128,16,2880]{2,1,0:T(8,128)(2,1)}, u32[]{:S(2)}, u32[]{:S(2)}) async-start(bf16[128,16,2880]{2,1,0:T(8,128)(2,1)} %bitcast.125), calls=%async_computation.2 | async-start | bytes 24117248 | tf_op jit(solution)/shard_map/all_to_all | solution.py:185
  401.0 237.1 %all-gather.9.cloned.1.call-start = ((), (), s32[]{:S(2)}) async-start(), calls=%async_computation.8 | async-start | bytes 3038208 | tf_op jit(solution)/shard_map/all_gather | solution.py:208
  559.4 7.9 %copy-start.7 = (f32[2880]{0:T(1024)S(1)}, f32[2880]{0:T(1024)}, u32[]{:S(2)}) copy-start(f32[2880]{0:T(1024)} %param.36) | copy-start | bytes 34564
  638.1 13.9 %copy-start.1 = (bf16[512,2880]{0,1:T(8,128)(2,1)S(1)}, bf16[512,2880]{0,1:T(8,128)(2,1)}, u32[]{:S(2)}) copy-start(bf16[512,2880]{0,1:T(8,128)(2,1)} %param.27) | copy-start | bytes 8847364
Sparse Core Ops, SparseCore 0:
  9.7 35.2 all-gather.4
  68.3 39.1 all-reduce.2
  110.1 33.2 reduce-scatter.1
  146.0 31.5 all-gather.6
  568.1 69.9 all-gather.8
where the time goes:
time: 668 us; the launch traced here: 659 us
  waiting for transfers between devices  322 us (48%)
  blocking collectives  157 us (24%)
  matrix products  68.2 us (10%)
  local copies, waits for them, and re-layouts  52.3 us (8%)
  other arithmetic  29 us (4%)
  starting transfers between devices  15.4 us (2%)
  between operations  14.3 us (2%)
    all_to_all x1, blocking collectives, shards(): lax.all_to_all(copies, ('dp', 'expert'), split_axis=0, concat_axis=0, til...  146 us
    all_to_all x1, waiting for transfers between devices, shards(): lax.all_to_all(shares_out, ('dp', 'expert'), split_axis=0, concat_axis=0,...  134 us
    all_gather x1, waiting for transfers between devices, shards(): spread_rows = lax.all_gather(ends, ('dp', 'expert'), axis=0, tiled=True)  57.2 us
    reduce_scatter x1, waiting for transfers between devices, shards(): lax.psum_scatter(partial_out.astype(jnp.bfloat16), 'dp', scatter_dimensio...  35.9 us
    psum x1, waiting for transfers between devices, shards(): lax.psum(jnp.dot(blended_hidden, output_down_maps, preferred_element_type...  35 us
    all_gather x1, waiting for transfers between devices, shards(): gathered_rows = lax.all_gather(hidden, 'dp', axis=1, tiled=True)  32.8 us
    dot_general x1, matrix products, shards(): jnp.dot(activated, down_weight, preferred_element_type=jnp.float32)  26.6 us
    all_gather x1, waiting for transfers between devices, shards(): column_full = lax.all_gather(resid, 'dp', axis=1, tiled=True)  26.5 us
  transfers between devices with their start and end apart: 6, of which 6 were waited for; matrix products, arithmetic and copies ran while one was open for 2% of the time, Pallas kernels for 0%

commit v1 on v0

v1 whole, which is shorter than its diff:
```python
import functools

import jax
import jax.numpy as jnp
from jax import lax
from jax.experimental import pallas as pl
from jax.experimental.pallas import tpu as pltpu
from jax.sharding import PartitionSpec as P

HEAD_SIZE = 64
QUERY_GROUP = 8
TOP = 4
ADAPTER_RANK = 16
REQS = 4
CAP = 16
CHUNKS = 4

epsilon = 1e-05
theta_base = 150000.0
adapter_scale = 2.0
glu_alpha = 1.702

MESH = pl.DeviceIdType.MESH
BF = jnp.bfloat16
F32 = jnp.float32
VMEM = pl.BlockSpec(memory_space=pltpu.VMEM)
ANY = pl.BlockSpec(memory_space=pl.ANY)


def dot(a, b):
    return jnp.dot(a, b, preferred_element_type=F32)


def place():
    z, n = lax.axis_index("dp"), lax.axis_size("dp")
    c, m = lax.axis_index("expert"), lax.axis_size("expert")
    return z, n, c, m


def greet_z(offsets):
    z, n, c, _ = place()
    barrier = pltpu.get_barrier_semaphore()
    for o in offsets:
        pl.semaphore_signal(barrier, inc=1, device_id=(lax.rem(z + o, n), c), device_id_type=MESH)
    pl.semaphore_wait(barrier, len(offsets))


def send(src, dst, send_sem, recv_sem, device):
    copy = pltpu.make_async_remote_copy(
        src_ref=src, dst_ref=dst, send_sem=send_sem, recv_sem=recv_sem, device_id=device, device_id_type=MESH
    )
    copy.start()
    return copy


def wait_bytes(ref, sem):
    pltpu.make_async_copy(ref, ref, sem).wait()


def gather_kernel(x_ref, a_ref, xo_ref, ao_ref, ss, rs, local):
    z, n, c, _ = place()
    greet_z((1, 2, 3))
    own = pltpu.make_async_copy(x_ref, xo_ref.at[z], local.at[0])
    own.start()
    own_a = pltpu.make_async_copy(a_ref, ao_ref.at[z], local.at[1])
    own_a.start()
    half = x_ref.shape[0] // 2
    zu, zd = lax.rem(z + 1, n), lax.rem(z + 3, n)
    up, down, far = (zu, c), (zd, c), (lax.rem(z + 2, n), c)
    lo, hi = pl.ds(0, half), pl.ds(half, half)
    copies = [
        send(x_ref.at[lo], xo_ref.at[z, lo], ss.at[0], rs.at[0], up),
        send(x_ref.at[hi], xo_ref.at[z, hi], ss.at[1], rs.at[1], down),
        send(a_ref, ao_ref.at[z], ss.at[6], rs.at[6], up),
        send(a_ref, ao_ref.at[z], ss.at[7], rs.at[7], down),
        send(a_ref, ao_ref.at[z], ss.at[8], rs.at[8], far),
        send(x_ref.at[hi], xo_ref.at[z, hi], ss.at[2], rs.at[2], up),
        send(x_ref.at[lo], xo_ref.at[z, lo], ss.at[3], rs.at[3], down),
    ]
    copies[0].wait_recv()
    copies.append(send(xo_ref.at[zd, lo], xo_ref.at[zd, lo], ss.at[4], rs.at[4], up))
    copies[1].wait_recv()
    copies.append(send(xo_ref.at[zu, hi], xo_ref.at[zu, hi], ss.at[5], rs.at[5], down))
    for copy in copies[2:]:
        copy.wait_recv()
    for copy in copies:
        copy.wait_send()
    own.wait()
    own_a.wait()


def gather_z(hidden, aux):
    n = lax.axis_size("dp")
    return pl.pallas_call(
        gather_kernel,
        out_shape=(
            jax.ShapeDtypeStruct((n,) + hidden.shape, hidden.dtype),
            jax.ShapeDtypeStruct((n,) + aux.shape, aux.dtype),
        ),
        in_specs=[VMEM, VMEM],
        out_specs=(VMEM, VMEM),
        scratch_shapes=[
            pltpu.SemaphoreType.DMA((9,)),
            pltpu.SemaphoreType.DMA((9,)),
            pltpu.SemaphoreType.DMA((2,)),
        ],
        compiler_params=pltpu.CompilerParams(
            collective_id=0, has_side_effects=True, vmem_limit_bytes=32 * 2**20
        ),
    )(hidden, aux)


def out_kernel(
    b_ref, wo_ref, odm_ref, hid_ref, mask_ref, oum_ref, gain_ref,
    resid_ref, moe_ref,
    low_snd, low_rcv, snd, rcv, st_snd, st_rcv, ss, rs,
):
    z, n, c, _ = place()
    blended = b_ref[...]
    low = dot(blended, odm_ref[...]).astype(BF)
    low_snd[...] = low
    greet_z((1, 2, 3))
    copies = []
    for o in (2, 1, 3):
        peer = (lax.rem(z + o, n), c)
        copies.append(send(low_snd, low_rcv.at[o - 1], ss.at[o - 1], rs.at[o - 1], peer))
    for o in (2, 1, 3):
        q = lax.rem(z + o, n)
        snd[o - 1] = dot(blended, wo_ref[q]).astype(BF)
        copies.append(send(snd.at[o - 1], rcv.at[o - 1], ss.at[o + 2], rs.at[o + 2], (q, c)))
    total = hid_ref[...].astype(F32) + dot(blended, wo_ref[z]).astype(BF).astype(F32)
    for copy in copies[:3]:
        copy.wait_recv()
    low_sum = low.astype(F32)
    for k in range(3):
        low_sum = low_sum + low_rcv[k].astype(F32)
    picked = (low_sum * mask_ref[...]).astype(BF)
    total = total + adapter_scale * dot(picked, oum_ref[...])
    for copy in copies[3:]:
        copy.wait_recv()
    for k in range(3):
        total = total + rcv[k].astype(F32)
    resid = total.astype(BF)
    resid_ref[...] = resid
    wide = resid.astype(F32)
    sums = jnp.sum(wide * wide, axis=1, keepdims=True)
    st_snd[...] = jnp.broadcast_to(sums, (sums.shape[0], 128)).T[:8]
    more = []
    for o in (2, 1, 3):
        more.append(send(st_snd, st_rcv.at[o - 1], ss.at[o + 5], rs.at[o + 5], (lax.rem(z + o, n), c)))
    for copy in more:
        copy.wait_recv()
    every = st_snd[...] + st_rcv[0] + st_rcv[1] + st_rcv[2]
    width = hid_ref.shape[1] * 4
    scale = lax.rsqrt(every / width + epsilon)
    column = jnp.concatenate([scale] * 16, axis=0).T[:, :1]
    moe_ref[...] = (wide * column * gain_ref[...]).astype(BF)
    for copy in copies + more:
        copy.wait_send()


def out_project(blended, wo4, odm, hidden, mask, oum, gain):
    rows, q = hidden.shape
    n = 3
    return pl.pallas_call(
        out_kernel,
        out_shape=(jax.ShapeDtypeStruct((rows, q), BF), jax.ShapeDtypeStruct((rows, q), BF)),
        in_specs=[VMEM] * 7,
        out_specs=(VMEM, VMEM),
        scratch_shapes=[
            pltpu.VMEM(mask.shape, BF),
            pltpu.VMEM((n,) + mask.shape, BF),
            pltpu.VMEM((n, rows, q), BF),
            pltpu.VMEM((n, rows, q), BF),
            pltpu.VMEM((8, rows), F32),
            pltpu.VMEM((n, 8, rows), F32),
            pltpu.SemaphoreType.DMA((9,)),
            pltpu.SemaphoreType.DMA((9,)),
        ],
        compiler_params=pltpu.CompilerParams(
            collective_id=1, has_side_effects=True, vmem_limit_bytes=48 * 2**20
        ),
    )(blended, wo4, odm, hidden, mask, oum, gain)


def expert_kernel(
    slots, d_ref, mi_ref, wg_hbm, wu_hbm, wd_hbm, out_hbm,
    mi_nb, stg, xb, wg, wu, wd, yo, ys, yr,
    w_sem, mi_sem, ds, dr, zs, zr, ps, pr, bs, br, own_sem,
):
    z, n, c, m = place()
    up, down = lax.rem(z + 1, n), lax.rem(z + 3, n)
    rows = slots * m
    per = m // CHUNKS
    span = per * slots
    q = mi_ref.shape[1]
    quarters = (z, down, up, lax.rem(z + 2, n))
    weights = []
    for r in range(4):
        at = pl.ds(pl.multiple_of(quarters[r] * q, 16), q)
        weights.append(pltpu.make_async_copy(wg_hbm.at[at], wg.at[r], w_sem.at[0, r]))
        weights.append(pltpu.make_async_copy(wu_hbm.at[at], wu.at[r], w_sem.at[1, r]))
        weights.append(pltpu.make_async_copy(wd_hbm.at[quarters[r]], wd.at[r], w_sem.at[2, r]))
    for w in weights:
        w.start()
    barrier = pltpu.get_barrier_semaphore()

    @pl.loop(1, m)
    def _(j):
        pl.semaphore_signal(barrier, inc=1, device_id=(z, lax.rem(c + j, m)), device_id_type=MESH)

    for peer in (up, down):
        pl.semaphore_signal(barrier, inc=1, device_id=(peer, c), device_id_type=MESH)
    pl.semaphore_wait(barrier, m + 1)
    first = send(mi_ref, mi_nb, mi_sem.at[0], mi_sem.at[1], (up, c))

    def chunk(ch):
        return pl.ds(ch * span, span)

    def dispatch(ch, r):
        source = mi_ref if r == 0 else mi_nb
        stg[r, chunk(ch)] = dot(d_ref[chunk(ch)], source[...]).astype(BF)

        @pl.loop(max(1, ch * per), (ch + 1) * per)
        def _(j):
            at = pl.ds(pl.multiple_of(j * slots, slots), slots)
            send(stg.at[r, at], xb.at[r, at], ds.at[r, ch], dr.at[r, ch], (z, lax.rem(c + j, m)))

        if ch == 0:
            xb[r, :slots] = stg[r, :slots]

    def but_own(ch):
        return pl.ds(slots, span - slots) if ch == 0 else chunk(ch)

    def forward(ch):
        wait_bytes(xb.at[0, but_own(ch)], dr.at[0, ch])
        send(xb.at[0, chunk(ch)], xb.at[2, chunk(ch)], zs.at[0, ch], zr.at[0, ch], (down, c))
        wait_bytes(xb.at[1, but_own(ch)], dr.at[1, ch])
        send(xb.at[1, chunk(ch)], xb.at[3, chunk(ch)], zs.at[1, ch], zr.at[1, ch], (up, c))

    tile = min(256, span)

    def experts(ch):
        wait_bytes(xb.at[2, chunk(ch)], zr.at[0, ch])
        wait_bytes(xb.at[3, chunk(ch)], zr.at[1, ch])

        @pl.loop(0, span // tile)
        def _(t):
            at = pl.ds(pl.multiple_of(ch * span + t * tile, tile), tile)
            gate = dot(xb[0, at], wg[0])
            for r in range(1, 4):
                gate = gate + dot(xb[r, at], wg[r])
            lift = dot(xb[0, at], wu[0])
            for r in range(1, 4):
                lift = lift + dot(xb[r, at], wu[r])
            act = (gate * jax.nn.sigmoid(glu_alpha * gate) * (lift + 1.0)).astype(BF)
            for r in range(2, 4):
                ys[r - 2, at] = dot(act, wd[r]).astype(BF)
            for r in range(2):
                yo[r, at] = dot(act, wd[r]).astype(BF)

        send(ys.at[0, chunk(ch)], yr.at[0, chunk(ch)], ps.at[0, ch], pr.at[0, ch], (up, c))
        send(ys.at[1, chunk(ch)], yr.at[1, chunk(ch)], ps.at[1, ch], pr.at[1, ch], (down, c))

    def give_back(ch):
        for r in range(2):
            wait_bytes(yr.at[r, chunk(ch)], pr.at[r, ch])
            yo[r, chunk(ch)] = (yo[r, chunk(ch)].astype(F32) + yr[r, chunk(ch)].astype(F32)).astype(BF)

            @pl.loop(max(1, ch * per), (ch + 1) * per)
            def _(j):
                at = pl.ds(pl.multiple_of(j * slots, slots), slots)
                send(yo.at[r, at], out_hbm.at[r, at], bs.at[r, ch], br.at[r, ch], (z, lax.rem(c + m - j, m)))

            if ch == 0:
                pltpu.make_async_copy(yo.at[r, pl.ds(0, slots)], out_hbm.at[r, pl.ds(0, slots)], own_sem.at[r]).start()

    dispatch(0, 0)
    dispatch(1, 0)
    first.wait_recv()
    dispatch(0, 1)
    dispatch(1, 1)
    for ch in range(2, CHUNKS):
        dispatch(ch, 0)
        dispatch(ch, 1)
    forward(0)
    for w in weights:
        w.wait()
    for ch in range(CHUNKS):
        if ch + 1 < CHUNKS:
            forward(ch + 1)
        experts(ch)
        if ch:
            give_back(ch - 1)
    give_back(CHUNKS - 1)
    first.wait_send()
    for r in range(2):
        for ch in range(CHUNKS):
            wait_bytes(stg.at[r, but_own(ch)], ds.at[r, ch])
            wait_bytes(xb.at[r, chunk(ch)], zs.at[r, ch])
            wait_bytes(ys.at[r, chunk(ch)], ps.at[r, ch])
            wait_bytes(yo.at[r, but_own(ch)], bs.at[r, ch])
            wait_bytes(out_hbm.at[r, but_own(ch)], br.at[r, ch])
        wait_bytes(out_hbm.at[r, pl.ds(0, slots)], own_sem.at[r])


def experts_call(pick, moe_in, wg, wu, wd4, slots):
    rows, q = pick.shape[0], moe_in.shape[1]
    f = wg.shape[1]
    dma = lambda *s: pltpu.SemaphoreType.DMA(s)
    big = lambda k: pltpu.VMEM((k, rows, q), BF)
    return pl.pallas_call(
        functools.partial(expert_kernel, slots),
        out_shape=jax.ShapeDtypeStruct((2, rows, q), BF),
        in_specs=[VMEM, VMEM, ANY, ANY, ANY],
        out_specs=ANY,
        scratch_shapes=[
            pltpu.VMEM(moe_in.shape, BF),
            big(2), big(4),
            pltpu.VMEM((4, q, f), BF), pltpu.VMEM((4, q, f), BF), pltpu.VMEM((4, f, q), BF),
            big(2), big(2), big(2),
            dma(3, 4), dma(2),
            dma(2, CHUNKS), dma(2, CHUNKS), dma(2, CHUNKS), dma(2, CHUNKS),
            dma(2, CHUNKS), dma(2, CHUNKS), dma(2, CHUNKS), dma(2, CHUNKS), dma(2),
        ],
        compiler_params=pltpu.CompilerParams(
            collective_id=2, has_side_effects=True, vmem_limit_bytes=62 * 2**20
        ),
    )(pick, moe_in, wg, wu, wd4)


def finish_kernel(m0_ref, m1_ref, resid_ref, out_ref, rcv, sem):
    z, n, c, _ = place()
    up, down = lax.rem(z + 1, n), lax.rem(z + 3, n)
    greet_z((1, 3))
    copy = send(m1_ref, rcv, sem.at[0], sem.at[1], (down, c))
    copy.wait_recv()
    moe = (m0_ref[...] + rcv[...].astype(F32)).astype(BF)
    out_ref[...] = (resid_ref[...].astype(F32) + moe.astype(F32)).astype(BF)
    copy.wait_send()


def finish(m0, m1, resid):
    return pl.pallas_call(
        finish_kernel,
        out_shape=jax.ShapeDtypeStruct(resid.shape, BF),
        in_specs=[VMEM] * 3,
        out_specs=VMEM,
        scratch_shapes=[pltpu.VMEM(resid.shape, BF), pltpu.SemaphoreType.DMA((2,))],
        compiler_params=pltpu.CompilerParams(
            collective_id=3, has_side_effects=True, vmem_limit_bytes=32 * 2**20
        ),
    )(m0, m1, resid)


def rms_scale(values, gain_row):
    mean_square = jnp.mean(values * values, axis=-1, keepdims=True)
    return values * lax.rsqrt(mean_square + epsilon) * gain_row


def rotate(values, cosine, sine):
    half = values.shape[-1] // 2
    first, second = values[..., :half], values[..., half:]
    return jnp.concatenate([first * cosine - second * sine, second * cosine + first * sine], axis=-1)


def attend_heads(queries, keys, values, segment_row, sink_row):
    tokens, group, head_dim = queries.shape
    scores = jnp.einsum("tgh,sh->gts", queries, keys, preferred_element_type=F32) * head_dim ** (-0.5)
    counter = jnp.arange(tokens, dtype=jnp.int32)
    allowed = (segment_row[:, None] == segment_row[None, :]) & (counter[None, :] <= counter[:, None])
    weights = jnp.where(allowed[None], jnp.exp(scores), 0.0)
    totals = jnp.sum(weights, axis=-1, keepdims=True) + jnp.exp(sink_row).reshape(group, 1, 1)
    probs = (weights / totals).astype(BF)
    blended = jnp.einsum("gts,sh->tgh", probs, values, preferred_element_type=F32)
    return blended.astype(BF).reshape(tokens, group * head_dim)


def shards(
    hidden, segments, request_adapter, routes, expert_gates, attention_gain, joined_weight, sinks,
    attention_out_weight, joined_down_maps, joined_up_maps, output_down_maps, output_up_maps,
    expert_norm_gain, expert_gate_weight, expert_up_weight, expert_down_weight, closing_gain, vocabulary_weight,
):
    groups, columns = lax.axis_size("dp"), lax.axis_size("expert")
    z, c = lax.axis_index("dp"), lax.axis_index("expert")
    segment_row, adapter_row = segments[0], request_adapter[0]
    tokens, quarter = hidden.shape
    width = quarter * groups
    share = tokens // groups
    aux = jnp.concatenate(
        [routes[0].astype(BF), expert_gates[0], jnp.zeros((share, 128 - 2 * TOP), BF)], axis=1
    )
    hid4, aux4 = gather_z(hidden, aux)
    rows = jnp.transpose(hid4, (1, 0, 2)).reshape(tokens, width)

    normed = rms_scale(rows.astype(F32), attention_gain).astype(BF)
    ranks = joined_down_maps.shape[1]
    projected = dot(normed, joined_weight.reshape(width, -1))
    low = dot(normed, joined_down_maps).astype(BF)
    request_ids = jnp.arange(REQS, dtype=jnp.int32)
    hits = segment_row[:, None] == request_ids[None, :]
    adapter = jnp.sum(jnp.where(hits, adapter_row[None, :], 0), axis=1)
    mask = adapter[:, None] == (jnp.arange(ranks, dtype=jnp.int32) // ADAPTER_RANK)[None, :]
    low = jnp.where(mask, low, jnp.zeros_like(low))
    projected = projected + adapter_scale * dot(low, joined_up_maps.reshape(ranks, -1))
    counter = jnp.arange(tokens, dtype=jnp.int32)
    starts = jnp.min(jnp.where(hits, counter[:, None], tokens), axis=0)
    positions = counter - jnp.sum(jnp.where(hits, starts[None, :], 0), axis=1)
    half = HEAD_SIZE // 2
    frequency = theta_base ** (-2.0 * jnp.arange(half, dtype=F32) / HEAD_SIZE)
    angles = positions.astype(F32)[:, None] * frequency[None, :]
    cosine, sine = jnp.cos(angles)[:, None, :], jnp.sin(angles)[:, None, :]
    projected = projected.reshape(tokens, QUERY_GROUP + 2, HEAD_SIZE)
    turned = rotate(projected[:, : QUERY_GROUP + 1], cosine, sine).astype(BF)
    blended = attend_heads(
        turned[:, :QUERY_GROUP], turned[:, QUERY_GROUP], projected[:, QUERY_GROUP + 1].astype(BF), segment_row, sinks
    )

    wo4 = jnp.transpose(attention_out_weight.reshape(-1, groups, quarter), (1, 0, 2))
    gain = lax.dynamic_slice_in_dim(expert_norm_gain, z * quarter, quarter)[None, :]
    resid, moe_in = out_project(
        blended, wo4, output_down_maps, hidden, mask.astype(F32), output_up_maps, gain
    )

    route_all = aux4[:, :, :TOP].reshape(tokens, TOP)
    gate_all = aux4[:, :, TOP : 2 * TOP].reshape(tokens, TOP)
    slots = CAP * groups
    targets = lax.rem(c + jnp.arange(columns, dtype=jnp.int32), columns).astype(BF)
    named = route_all[:, :, None] == targets[None, None, :]
    hit = jnp.any(named, axis=1)
    gate_of = jnp.sum(jnp.where(named, gate_all.astype(F32)[:, :, None], 0.0), axis=1)
    before = (counter[None, :] < counter[:, None]).astype(BF)
    rank = jnp.where(hit, dot(before, hit.astype(BF)), -1.0)
    slot_ids = jnp.arange(slots, dtype=F32)
    pick = (rank.T[:, None, :] == slot_ids[None, :, None]).astype(BF).reshape(columns * slots, tokens)
    weigh = jnp.where(rank[:, :, None] == slot_ids[None, None, :], gate_of[:, :, None], 0.0)
    weigh = weigh.astype(BF).reshape(tokens, columns * slots)

    wd4 = jnp.transpose(expert_down_weight[0].reshape(-1, groups, quarter), (1, 0, 2))
    answers = experts_call(pick, moe_in, expert_gate_weight[0], expert_up_weight[0], wd4, slots)
    m0 = dot(weigh, answers[0])
    m1 = dot(weigh, answers[1]).astype(BF)
    hidden_out = finish(m0, m1, resid)

    last = jnp.max(jnp.where(hits, counter[:, None], -1), axis=0)
    chosen = jnp.take(hidden_out, last, axis=0)
    spread = lax.all_gather(chosen, ("dp", "expert"), axis=0, tiled=True)
    ends = jnp.transpose(spread.reshape(groups, columns * REQS, quarter), (1, 0, 2)).reshape(-1, width)
    ends = rms_scale(ends.astype(F32), closing_gain).astype(BF)
    logits = dot(ends, vocabulary_weight)
    return hidden_out, logits


def solution(mesh):
    in_specs = (
        P("expert", "dp"),
        P("expert", None),
        P("expert", None),
        P("expert", "dp", None),
        P("expert", "dp", None),
        P(),
        P(None, "dp", None),
        P("dp"),
        P("dp", None),
        P(),
        P(None, "dp", None),
        P("dp", None),
        P(None, "dp"),
        P(),
        P("expert", None, "dp"),
        P("expert", None, "dp"),
        P("expert", "dp", None),
        P(),
        P(None, ("dp", "expert")),
    )
    out_specs = (P("expert", "dp"), P(None, ("dp", "expert")))
    return jax.shard_map(shards, mesh=mesh, in_specs=in_specs, out_specs=out_specs, check_vma=False)
```

time: 668 us -> 492 us (0.74)
  Pallas kernels: 0 us -> 345 us
  waiting for transfers between devices: 322 us -> 0 us
  blocking collectives: 157 us -> 40.4 us
  matrix products: 68.2 us -> 23.4 us
  starting transfers between devices: 15.4 us -> 0 us
  other arithmetic: 29 us -> 15.1 us
  between operations: 14.3 us -> 1.27 us
    pallas_call x0 -> x4, Pallas kernels: none -> 345 us  [the longest x1 268 us: experts_call(): pl.pallas_call(functools.partial(expert_kernel, slots), out_shape=jax.Sha...]
    all_to_all x2 -> x0, blocking collectives: 157 us -> none  [the longest x1 146 us: shards(): lax.all_to_all(copies, ('dp', 'expert'), split_axis=0, concat_axis=0, til...]
    all_to_all x1 -> x0, waiting for transfers between devices: 134 us -> none  [shards(): lax.all_to_all(shares_out, ('dp', 'expert'), split_axis=0, concat_axis=0,...]
    all_gather x3 -> x0, waiting for transfers between devices: 117 us -> none  [the longest x1 57.2 us: shards(): spread_rows = lax.all_gather(ends, ('dp', 'expert'), axis=0, tiled=True)]
    dot_general x10 -> x8, matrix products: 68.2 us -> 23.4 us  [the longest x6 20.8 us: dot(): return jnp.dot(a, b, preferred_element_type=F32)]
    all_gather x0 -> x1, blocking collectives: none -> 40.4 us  [shards(): spread = lax.all_gather(chosen, ('dp', 'expert'), axis=0, tiled=True)]
    reduce_scatter x1 -> x0, waiting for transfers between devices: 35.9 us -> none  [shards(): lax.psum_scatter(partial_out.astype(jnp.bfloat16), 'dp', scatter_dimensio...]
    psum x1 -> x0, waiting for transfers between devices: 35 us -> none  [shards(): lax.psum(jnp.dot(blended_hidden, output_down_maps, preferred_element_type...]
  transfers between devices with their start and end apart: 6 -> 0, of which waited for: 6 -> 0; matrix products, arithmetic and copies ran while one was open for 2% -> 0% of each run, Pallas kernels for 0% -> 0%
where the time goes in v1:
time: 492 us; the launch traced here: 483 us
  Pallas kernels  345 us (70%)
  local copies, waits for them, and re-layouts  57.9 us (12%)
  blocking collectives  40.4 us (8%)
  matrix products  23.4 us (5%)
  other arithmetic  15.1 us (3%)
    pallas_call x1, Pallas kernels, experts_call(): pl.pallas_call(functools.partial(expert_kernel, slots), out_shape=jax.Sha...  268 us
    all_gather x1, blocking collectives, shards(): spread = lax.all_gather(chosen, ('dp', 'expert'), axis=0, tiled=True)  40.4 us
    pallas_call x1, Pallas kernels, out_project(): pl.pallas_call(out_kernel, out_shape=(jax.ShapeDtypeStruct((rows, q), BF)...  36.8 us
    unnamed x38, local copies, waits for them, and re-layouts  27.5 us
    pallas_call x1, Pallas kernels, gather_z(): pl.pallas_call(gather_kernel, out_shape=(jax.ShapeDtypeStruct((n,) + hidd...  25.6 us
    dot_general x6, matrix products, dot(): return jnp.dot(a, b, preferred_element_type=F32)  20.8 us
    pallas_call x1, Pallas kernels, finish(): pl.pallas_call(finish_kernel, out_shape=jax.ShapeDtypeStruct(resid.shape,...  15.1 us

profile of v1, /device:TPU:1, one launch (start us, length us, event | category | flops | bytes accessed | tf_op | source)
XLA Modules:
  0.0 483.3 jit_solution(16376240283148325339)
XLA Ops:
  0.6 2.2 copy.98.x_ref.hid_ref
  3.6 0.8 copy.97
  4.6 1.1 copy-done.3
  5.7 25.6 %shard_map.194 = (bf16[4,384,720]{2,1,0:T(8,128)(2,1)S(1)}, bf16[4,96,128]{2,1,0:T(8,128)(2,1)S(1)}) custom-call(bf16[384,720]{1,0:T(8,128)(2,1)S(1)} %copy-done.3, bf16[96,128]{1,0:T(8,128)(2,1)S(1)} %maximum_maximum_fusion.a_ref), custom_call_target="tpu_custom_call" | custom-call | tf_op jit(solution)/shard_map/pallas_call | solution.py:94
  31.9 2.5 convert_bitcast_fusion
  34.4 6.0 %copy.102 = f32[384,4,720]{0,2,1:T(8,128)} copy(f32[384,4,720]{2,0,1:T(8,128)} %convert_bitcast_fusion) | data formatting | bytes 8847360 | tf_op jit(solution)/shard_map/convert_element_type | solution.py:396
  40.4 4.1 fusion.4
  44.6 2.1 fusion.15
  46.7 4.3 copy.101
  51.0 5.8 %fusion.6 = f32[384,640]{1,0:T(8,128)} fusion(bf16[384,2880]{0,1:T(8,128)(2,1)} %bitcast.98, bf16[2880,1,640]{2,0,1:T(8,128)(2,1)} %param.25), kind=kOutput, calls=%fused_computation.13 | convolution fusion | flops 1415577600 | bytes 6881280 | tf_op jit(solution)/shard_map/dot_general | solution.py:31
  57.2 3.3 fusion.19
  60.5 1.5 copy.103
  62.6 1.3 fusion.5
  64.0 1.3 fusion.23
  66.4 5.2 %copy.105 = bf16[512,4,720]{2,0,1:T(8,128)(2,1)} copy(bf16[512,4,720]{0,2,1:T(8,128)(2,1)} %bitcast.97) | data formatting | bytes 5898240 | tf_op jit(solution)/shard_map/reshape | solution.py:419
  71.8 1.9 copy-done.2
  73.7 36.8 %shard_map.195 = (bf16[384,720]{1,0:T(8,128)(2,1)S(1)}, bf16[384,720]{1,0:T(8,128)(2,1)S(1)}) custom-call(bf16[384,512]{1,0:T(8,128)(2,1)S(1)} %copy.106.b_ref, bf16[4,512,720]{2,1,0:T(8,128)(2,1)S(1)} %bitcast.89, bf16[512,128]{1,0:T(8,128)(2,1)S(1)} %copy-done.6, bf16[384,720]{1,0:T(8,128)(2,1)S(1)} %copy-done.4, ...), custom_call_target="tpu_custom_call" | custom-call | tf_op jit(solution)/shard_map/pallas_call | solution.py:165
  111.1 1.5 fusion.14.d_ref
  112.6 6.5 %copy.111 = bf16[1,720,2880]{1,2,0:T(8,128)(2,1)} copy(bf16[1,720,2880]{2,1,0:T(8,128)(2,1)} %param.35) | data formatting | bytes 8294400 | tf_op args[16]
  119.2 6.5 %copy.112 = bf16[720,4,720]{2,0,1:T(8,128)(2,1)} copy(bf16[720,4,720]{0,2,1:T(8,128)(2,1)} %bitcast.93) | data formatting | bytes 8294400 | tf_op jit(solution)/shard_map/reshape;squeeze | solution.py:439
  125.7 6.5 %copy.109 = bf16[1,2880,720]{2,1,0:T(8,128)(2,1)} copy(bf16[1,2880,720]{1,2,0:T(8,128)(2,1)} %param.33) | data formatting | bytes 8294400 | tf_op args[14]
  132.1 6.5 %copy.110 = bf16[1,2880,720]{2,1,0:T(8,128)(2,1)} copy(bf16[1,2880,720]{1,2,0:T(8,128)(2,1)} %param.34) | data formatting | bytes 8294400 | tf_op args[15]
  138.7 267.6 %shard_map.196 = bf16[2,2048,720]{2,1,0:T(8,128)(2,1)} custom-call(bf16[2048,384]{1,0:T(8,128)(2,1)} %fusion.14.d_ref, bf16[384,720]{1,0:T(8,128)(2,1)} %copy-done.5, bf16[2880,720]{1,0:T(8,128)(2,1)} %bitcast.91, bf16[2880,720]{1,0:T(8,128)(2,1)} %bitcast.92, bf16[4,720,720]{2,1,0:T(8,128)(2,1)} %bitcast.90), custom_call_target="tpu_custom_call" | custom-call | tf_op jit(solution)/shard_map/pallas_call | solution.py:312
  407.0 3.6 fusion.20
  410.9 3.3 fusion.10.m0_ref
  414.2 15.1 %shard_map.197 = bf16[384,720]{1,0:T(8,128)(2,1)S(1)} custom-call(f32[384,720]{1,0:T(8,128)S(1)} %fusion.10.m0_ref, bf16[384,720]{1,0:T(8,128)(2,1)S(1)} %copy.114.m1_ref, bf16[384,720]{1,0:T(8,128)(2,1)S(1)} %get-tuple-element.9.resid_ref), custom_call_target="tpu_custom_call" | custom-call | tf_op jit(solution)/shard_map/pallas_call | solution.py:344
  430.0 40.4 %all-gather = bf16[128,4,720]{2,1,0:T(4,128)(2,1)S(1)} all-gather(bf16[1,4,720]{2,1,0:T(4,128)(2,1)S(1)} %select_bitcast_fusion), channel_id=1, replica_groups=mesh['dp'=4,'expert'=32] {'dp','expert'}, dimensions={0}, use_global_device_ids=true | all-gather | bytes 743040 | tf_op jit(solution)/shard_map/all_gather | solution.py:447
  470.5 1.5 reshape.314
  471.9 3.0 copy.115
  475.6 1.9 fusion.18
  477.5 4.5 fusion.46
  482.0 1.0 copy.116
  (73 shorter events, 6.6 us)
Async XLA Ops:
  0.6 56.5 %copy-start = (bf16[2880,128]{1,0:T(8,128)(2,1)S(1)}, bf16[2880,128]{1,0:T(8,128)(2,1)}, u32[]{:S(2)}) copy-start(bf16[2880,128]{1,0:T(8,128)(2,1)} %param.28) | copy-start | bytes 2211844
  4.6 1.1 copy-start.3
  34.4 6.0 %copy-start.10 = (f32[2880]{0:T(1024)S(1)}, f32[2880]{0:T(1024)}, u32[]{:S(2)}) copy-start(f32[2880]{0:T(1024)} %param.24) | copy-start | bytes 34564
  51.0 5.8 %copy-start.12 = (s32[1,384]{1,0:T(1,128)S(1)}, s32[1,384]{1,0:T(1,128)}, u32[]{:S(2)}) copy-start(s32[1,384]{1,0:T(1,128)} %param.20) | copy-start | bytes 4612
  51.0 6.0 %copy-start.13 = (s32[1,4]{1,0:T(1,128)S(1)}, s32[1,4]{1,0:T(1,128)}, u32[]{:S(2)}) copy-start(s32[1,4]{1,0:T(1,128)} %param.21) | copy-start | bytes 52
  51.0 6.1 %copy-start.7 = (bf16[384,2880]{0,1:T(8,128)(2,1)S(1)}, bf16[384,2880]{0,1:T(8,128)(2,1)}, u32[]{:S(2)}) copy-start(bf16[384,2880]{0,1:T(8,128)(2,1)} %fusion.4) | copy-start | bytes 6635524
  51.0 6.2 %copy-start.9 = (bf16[128,1,640]{2,0,1:T(8,128)(2,1)S(1)}, bf16[128,1,640]{2,0,1:T(8,128)(2,1)}, u32[]{:S(2)}) copy-start(bf16[128,1,640]{2,0,1:T(8,128)(2,1)} %param.29) | copy-start | bytes 491524
  62.6 1.3 copy-start.14
  66.3 5.3 %copy-start.8 = (bf16[128,720]{0,1:T(8,128)(2,1)S(1)}, bf16[128,720]{0,1:T(8,128)(2,1)}, u32[]{:S(2)}) copy-start(bf16[128,720]{0,1:T(8,128)(2,1)} %param.31) | copy-start | bytes 552964
  66.4 5.4 %copy-start.4 = (bf16[384,720]{1,0:T(8,128)(2,1)S(1)}, bf16[384,720]{1,0:T(8,128)(2,1)}, u32[]{:S(2)}) copy-start(bf16[384,720]{1,0:T(8,128)(2,1)} %copy.98.x_ref.hid_ref) | copy-start | bytes 1658884
  66.4 5.4 %copy-start.6 = (bf16[512,128]{1,0:T(8,128)(2,1)S(1)}, bf16[512,128]{1,0:T(8,128)(2,1)}, u32[]{:S(2)}) copy-start(bf16[512,128]{1,0:T(8,128)(2,1)} %odm_ref.1) | copy-start | bytes 393220
  71.8 1.9 copy-start.2
  110.5 8.6 %copy-start.5 = (bf16[384,720]{1,0:T(8,128)(2,1)}, bf16[384,720]{1,0:T(8,128)(2,1)S(1)}, u32[]{:S(2)}) copy-start(bf16[384,720]{1,0:T(8,128)(2,1)S(1)} %get-tuple-element.8.mi_ref) | copy-start | bytes 1658884
  470.5 5.1 %copy-start.11 = (f32[2880]{0:T(1024)S(1)}, f32[2880]{0:T(1024)}, u32[]{:S(2)}) copy-start(f32[2880]{0:T(1024)} %param.36) | copy-start | bytes 34564
  475.6 7.4 %copy-start.1 = (bf16[2880,128]{1,0:T(8,128)(2,1)S(1)}, bf16[2880,128]{1,0:T(8,128)(2,1)}, u32[]{:S(2)}) copy-start(bf16[2880,128]{1,0:T(8,128)(2,1)} %param.28) | copy-start | bytes 2211844

commit v2 on v1

v2 whole, which is shorter than its diff:
```python
import functools

import jax
import jax.numpy as jnp
from jax import lax
from jax.experimental import pallas as pl
from jax.experimental.pallas import tpu as pltpu
from jax.sharding import PartitionSpec as P

HEAD_SIZE = 64
QUERY_GROUP = 8
TOP = 4
ADAPTER_RANK = 16
REQS = 4
CAP = 16
CHUNKS = 8
PER = 4
EARLY = 4
AHEAD = 2
BACK = 1
ABSORB = 2
SENDING = 5
RING = 3

epsilon = 1e-05
theta_base = 150000.0
adapter_scale = 2.0
glu_alpha = 1.702

MESH = pl.DeviceIdType.MESH
BF = jnp.bfloat16
F32 = jnp.float32
VMEM = pl.BlockSpec(memory_space=pltpu.VMEM)
ANY = pl.BlockSpec(memory_space=pl.ANY)


def dot(a, b):
    return jnp.dot(a, b, preferred_element_type=F32)


def dot_nt(a, b):
    return lax.dot_general(a, b, (((1,), (1,)), ((), ())), preferred_element_type=F32)


def dot_tn(a, b):
    return lax.dot_general(a, b, (((0,), (0,)), ((), ())), preferred_element_type=F32)


def place():
    z, n = lax.axis_index("dp"), lax.axis_size("dp")
    c, m = lax.axis_index("expert"), lax.axis_size("expert")
    return z, n, c, m


def greet_z(offsets):
    z, n, c, _ = place()
    barrier = pltpu.get_barrier_semaphore()
    for o in offsets:
        pl.semaphore_signal(barrier, inc=1, device_id=(lax.rem(z + o, n), c), device_id_type=MESH)
    pl.semaphore_wait(barrier, len(offsets))


def send(src, dst, send_sem, recv_sem, device):
    copy = pltpu.make_async_remote_copy(
        src_ref=src, dst_ref=dst, send_sem=send_sem, recv_sem=recv_sem, device_id=device, device_id_type=MESH
    )
    copy.start()
    return copy


def wait_bytes(ref, sem):
    pltpu.make_async_copy(ref, ref, sem).wait()


def gather_kernel(x_ref, a_ref, xo_ref, ao_ref, ss, rs, local):
    z, n, c, _ = place()
    greet_z((1, 2, 3))
    own = pltpu.make_async_copy(x_ref, xo_ref.at[z], local.at[0])
    own.start()
    own_a = pltpu.make_async_copy(a_ref, ao_ref.at[z], local.at[1])
    own_a.start()
    half = x_ref.shape[0] // 32 * 16
    zu, zd = lax.rem(z + 1, n), lax.rem(z + 3, n)
    up, down, far = (zu, c), (zd, c), (lax.rem(z + 2, n), c)
    lo, hi = pl.ds(0, half), pl.ds(half, x_ref.shape[0] - half)
    copies = [
        send(x_ref.at[lo], xo_ref.at[z, lo], ss.at[0], rs.at[0], up),
        send(x_ref.at[hi], xo_ref.at[z, hi], ss.at[1], rs.at[1], down),
        send(a_ref, ao_ref.at[z], ss.at[6], rs.at[6], up),
        send(a_ref, ao_ref.at[z], ss.at[7], rs.at[7], down),
        send(a_ref, ao_ref.at[z], ss.at[8], rs.at[8], far),
        send(x_ref.at[hi], xo_ref.at[z, hi], ss.at[2], rs.at[2], up),
        send(x_ref.at[lo], xo_ref.at[z, lo], ss.at[3], rs.at[3], down),
    ]
    copies[0].wait_recv()
    copies.append(send(xo_ref.at[zd, lo], xo_ref.at[zd, lo], ss.at[4], rs.at[4], up))
    copies[1].wait_recv()
    copies.append(send(xo_ref.at[zu, hi], xo_ref.at[zu, hi], ss.at[5], rs.at[5], down))
    for copy in copies[2:]:
        copy.wait_recv()
    for copy in copies:
        copy.wait_send()
    own.wait()
    own_a.wait()


def gather_z(hidden, aux):
    n = lax.axis_size("dp")
    return pl.pallas_call(
        gather_kernel,
        out_shape=(
            jax.ShapeDtypeStruct((n,) + hidden.shape, hidden.dtype),
            jax.ShapeDtypeStruct((n,) + aux.shape, aux.dtype),
        ),
        in_specs=[VMEM, VMEM],
        out_specs=(VMEM, VMEM),
        scratch_shapes=[
            pltpu.SemaphoreType.DMA((9,)),
            pltpu.SemaphoreType.DMA((9,)),
            pltpu.SemaphoreType.DMA((2,)),
        ],
        compiler_params=pltpu.CompilerParams(
            collective_id=0, has_side_effects=True, vmem_limit_bytes=32 * 2**20
        ),
    )(hidden, aux)


def out_kernel(
    b_ref, wo_ref, odm_ref, hid_ref, mask_ref, oum_ref, gain_ref,
    resid_ref, moe_ref,
    low_snd, low_rcv, snd, rcv, st_snd, st_rcv, ss, rs,
):
    z, n, c, _ = place()
    quarter = hid_ref.shape[0]
    blended = b_ref[...]

    def part(q):
        return dot(wo_ref[pl.ds(pl.multiple_of(q * quarter, 16), quarter)], blended).astype(BF)

    low = dot_tn(odm_ref[...], blended).astype(BF)
    low_snd[...] = low
    greet_z((1, 2, 3))
    copies = []
    for o in (2, 1, 3):
        q = lax.rem(z + o, n)
        snd[o - 1] = part(q)
        copies.append(send(snd.at[o - 1], rcv.at[o - 1], ss.at[o + 2], rs.at[o + 2], (q, c)))
        copies.append(send(low_snd, low_rcv.at[o - 1], ss.at[o - 1], rs.at[o - 1], (q, c)))
    total = hid_ref[...].astype(F32) + part(z).astype(F32)
    for copy in copies[1::2]:
        copy.wait_recv()
    low_sum = low.astype(F32)
    for k in range(3):
        low_sum = low_sum + low_rcv[k].astype(F32)
    picked = (low_sum * mask_ref[...]).astype(BF)
    total = total + adapter_scale * dot(oum_ref[...], picked)
    for copy in copies[0::2]:
        copy.wait_recv()
    for k in range(3):
        total = total + rcv[k].astype(F32)
    resid = total.astype(BF)
    resid_ref[...] = resid
    wide = resid.astype(F32)
    sums = jnp.sum(wide * wide, axis=0, keepdims=True)
    st_snd[...] = jnp.broadcast_to(sums, st_snd.shape)
    more = []
    for o in (2, 1, 3):
        more.append(send(st_snd, st_rcv.at[o - 1], ss.at[o + 5], rs.at[o + 5], (lax.rem(z + o, n), c)))
    for copy in more:
        copy.wait_recv()
    every = st_snd[...] + st_rcv[0] + st_rcv[1] + st_rcv[2]
    scale = lax.rsqrt(every / (4.0 * quarter) + epsilon)
    moe_ref[...] = (wide * scale[:1] * gain_ref[...]).astype(BF)
    for copy in copies + more:
        copy.wait_send()


def out_project(blended, wo, odm, hidden, mask, oum, gain):
    q, rows = hidden.shape
    n = 3
    return pl.pallas_call(
        out_kernel,
        out_shape=(jax.ShapeDtypeStruct((q, rows), BF), jax.ShapeDtypeStruct((q, rows), BF)),
        in_specs=[VMEM] * 7,
        out_specs=(VMEM, VMEM),
        scratch_shapes=[
            pltpu.VMEM(mask.shape, BF),
            pltpu.VMEM((n,) + mask.shape, BF),
            pltpu.VMEM((n, q, rows), BF),
            pltpu.VMEM((n, q, rows), BF),
            pltpu.VMEM((8, rows), F32),
            pltpu.VMEM((n, 8, rows), F32),
            pltpu.SemaphoreType.DMA((9,)),
            pltpu.SemaphoreType.DMA((9,)),
        ],
        compiler_params=pltpu.CompilerParams(
            collective_id=1, has_side_effects=True, vmem_limit_bytes=48 * 2**20
        ),
    )(blended, wo, odm, hidden, mask, oum, gain)


def shift_of(j):
    s, dx = j // PER, j % PER
    return dx, (dx + s // 2) % 4, s % 2


def shifted(c, j, way):
    dx, dy, dk = shift_of(j)
    x, y, k = c // 8, (c // 2) % 4, c % 2
    return (((x + way * dx + 4) % 4) * 4 + (y + way * dy + 4) % 4) * 2 + (k + dk) % 2


def expert_kernel(
    slots, d_ref, g_ref, e_ref, mi_ref, resid_ref, wg_hbm, wu_hbm, wd_hbm,
    out_ref, spread_ref,
    mi_nb, stg, xb, wg, wu, wd, raw, yo, ys, yr, ans, macc, m1s, m1r, pk,
    w_sem, mi_sem, ds, dr, zs, zr, ps, pr, bs, br, own_sem, m_sem, ks, kr, ss, sr,
):
    z, n, c, m = place()
    span = PER * slots
    q = mi_ref.shape[0]

    def step(ch):
        return 1 + 2 * lax.rem(c + ch, 2)

    def near(ch):
        return lax.rem(z + step(ch), n)

    def away(ch):
        return lax.rem(z + 4 - step(ch), n)

    def quarters(ch):
        return z, away(ch), near(ch), lax.rem(z + 2, n)

    barrier = pltpu.get_barrier_semaphore()

    @pl.loop(1, m)
    def _(j):
        pl.semaphore_signal(barrier, inc=1, device_id=(z, lax.rem(c + j, m)), device_id_type=MESH)

    for o in (1, 2, 3):
        pl.semaphore_signal(barrier, inc=1, device_id=(lax.rem(z + o, n), c), device_id_type=MESH)
    pl.semaphore_wait(barrier, m + 2)
    first = send(mi_ref, mi_nb, mi_sem.at[0], mi_sem.at[1], (near(0), c))

    def block(j):
        return pl.ds(pl.multiple_of(j * slots, slots), slots)

    def chunk(ch):
        return pl.ds(pl.multiple_of(ch * span, span), span)

    def sent_in_plane(ring, sem, r, ch):
        @pl.when(ch == 0)
        def _():
            wait_bytes(ring.at[r, 0, pl.ds(0, span - slots)], sem.at[r, ch])

        @pl.when(ch != 0)
        def _():
            wait_bytes(ring.at[r, 0], sem.at[r, ch])

    def others(ch):
        return 1 - (ch + CHUNKS - 1) // CHUNKS

    def dispatch(ch, r):
        slot = lax.rem(ch, SENDING)
        source = mi_ref if r == 0 else mi_nb

        @pl.when(ch >= SENDING)
        def _():
            sent_in_plane(stg, ds, r, ch - SENDING)

        stg[r, slot] = dot_nt(d_ref[chunk(ch)], source[...]).astype(BF)

        @pl.loop(others(ch), PER)
        def _(a):
            j = ch * PER + a
            send(stg.at[r, slot, block(a)], xb.at[r, block(j)], ds.at[r, ch], dr.at[r, ch], (z, shifted(c, j, 1)))

        @pl.when(ch == 0)
        def _():
            xb[r, :slots] = stg[r, 0, :slots]

    def came_in_plane(buffer, sem, r, ch):
        @pl.when(ch == 0)
        def _():
            wait_bytes(buffer.at[r, pl.ds(slots, span - slots)], sem.at[r, ch])

        @pl.when(ch != 0)
        def _():
            wait_bytes(buffer.at[r, chunk(ch)], sem.at[r, ch])

    def forward(ch):
        came_in_plane(xb, dr, 0, ch)
        send(xb.at[0, chunk(ch)], xb.at[2, chunk(ch)], zs.at[0, ch], zr.at[0, ch], (away(ch), c))
        came_in_plane(xb, dr, 1, ch)
        send(xb.at[1, chunk(ch)], xb.at[3, chunk(ch)], zs.at[1, ch], zr.at[1, ch], (near(ch), c))

    def experts(ch):
        slot = lax.rem(ch, RING)
        at = chunk(ch)
        names = quarters(ch)

        def rows_of(r):
            return pl.ds(pl.multiple_of(names[r] * q, 16), q)

        for r in range(2):
            wait_bytes(xb.at[r + 2, at], zr.at[r, ch])

            @pl.when(ch >= RING)
            def _():
                wait_bytes(ys.at[r, 0], ps.at[r, ch - RING])
                sent_in_plane(yo, bs, r, ch - RING)

        gate = dot(xb[0, at], wg[rows_of(0)])
        for r in range(1, 4):
            gate = gate + dot(xb[r, at], wg[rows_of(r)])
        lift = dot(xb[0, at], wu[rows_of(0)])
        for r in range(1, 4):
            lift = lift + dot(xb[r, at], wu[rows_of(r)])
        act = (gate * jax.nn.sigmoid(glu_alpha * gate) * (lift + 1.0)).astype(BF)
        for r in range(2):
            ys[r, slot] = dot(act, wd[names[r + 2]]).astype(BF)
            send(ys.at[r, slot], yr.at[r, at], ps.at[r, ch], pr.at[r, ch], ((near(ch), away(ch))[r], c))
        for r in range(2):
            yo[r, slot] = dot(act, wd[names[r]]).astype(BF)

    def give_back(ch):
        slot = lax.rem(ch, RING)
        for r in range(2):
            wait_bytes(yr.at[r, chunk(ch)], pr.at[r, ch])
            yo[r, slot] = (yo[r, slot].astype(F32) + yr[r, chunk(ch)].astype(F32)).astype(BF)

            @pl.loop(others(ch), PER)
            def _(a):
                j = ch * PER + a
                send(yo.at[r, slot, block(a)], ans.at[r, block(j)], bs.at[r, ch], br.at[r, ch], (z, shifted(c, j, -1)))

            @pl.when(ch == 0)
            def _():
                ans[r, :slots] = yo[r, 0, :slots]

    def absorb(ch):
        for r in (1, 0):
            came_in_plane(ans, br, r, ch)
            macc[r] += dot(g_ref[:, chunk(ch)], ans[r, chunk(ch)])

    steps = [(w, h0, min(128, q - h0)) for w in range(3) for h0 in range(0, q, 128)]

    def fetch(i):
        w, h0, hs = steps[i]
        return pltpu.make_async_copy(
            (wg_hbm, wu_hbm, wd_hbm)[w].at[pl.ds(h0, hs)], raw.at[i % 2, pl.ds(0, hs)], w_sem.at[i % 2]
        )

    fetch(0).start()

    @pl.loop(0, EARLY)
    def _(ch):
        dispatch(ch, 0)

    macc[...] = jnp.zeros_like(macc)
    first.wait_recv()

    @pl.loop(0, EARLY)
    def _(ch):
        dispatch(ch, 1)

    for i, (w, h0, hs) in enumerate(steps):
        if i + 1 < len(steps):
            fetch(i + 1).start()
        fetch(i).wait()
        if w < 2:
            into = (wg, wu)[w]
            whole = 4 * q // 128

            @pl.loop(0, whole)
            def _(b):
                lanes = pl.ds(pl.multiple_of(b * 128, 128), 128)
                into[lanes, h0 : h0 + hs] = raw[i % 2, :hs, lanes].T

            rest = whole * 128
            if rest < 4 * q:
                into[rest : 4 * q, h0 : h0 + hs] = raw[i % 2, :hs, rest : 4 * q].T
        else:
            for f in range(4):
                wd[f, h0 : h0 + hs, :] = raw[i % 2, :hs, f * q : (f + 1) * q]

    @pl.loop(0, CHUNKS + AHEAD + BACK)
    def _(t):
        @pl.when(t < CHUNKS)
        def _():
            forward(t)

        @pl.when(t + EARLY < CHUNKS)
        def _():
            dispatch(t + EARLY, 0)
            dispatch(t + EARLY, 1)

        @pl.when((t >= AHEAD) & (t < CHUNKS + AHEAD))
        def _():
            experts(t - AHEAD)

        @pl.when(t >= AHEAD + BACK)
        def _():
            give_back(t - AHEAD - BACK)

        @pl.when(t >= AHEAD + BACK + ABSORB)
        def _():
            absorb(t - AHEAD - BACK - ABSORB)

    @pl.loop(CHUNKS - ABSORB, CHUNKS)
    def _(ch):
        absorb(ch)

    m1s[...] = macc[1].astype(BF)
    last = send(m1s, m1r, m_sem.at[0], m_sem.at[1], (away(0), c))
    last.wait_recv()
    moe = (macc[0] + m1r[...].astype(F32)).astype(BF)
    done = (resid_ref[...].astype(F32) + moe.T.astype(F32)).astype(BF)
    out_ref[...] = done

    ends = dot_nt(e_ref[...], done)
    ends = jnp.concatenate([ends, jnp.zeros((ends.shape[0], 768 - q), F32)], axis=1)
    piece = lax.broadcasted_iota(jnp.int32, (ends.shape[0], 256), 0) // REQS
    packed = jnp.where(piece == 0, ends[:, :256], jnp.where(piece == 1, ends[:, 256:512], ends[:, 512:]))
    pk[z] = packed.astype(BF)
    more = [send(pk.at[z], pk.at[z], ks.at[o - 1], kr.at[o - 1], (lax.rem(z + o, n), c)) for o in (2, 1, 3)]
    for copy in more:
        copy.wait_recv()
    chip, core = c // 2, c % 2
    own_ends = pltpu.make_async_copy(pk, spread_ref.at[core, chip], own_sem.at[0])
    own_ends.start()

    @pl.loop(1, m // 2)
    def _(j):
        there = (((chip // 4 + j // 4) % 4) * 4 + (chip + j) % 4) * 2 + core
        send(pk, spread_ref.at[core, chip], ss.at[0], sr.at[0], (z, there))

    own_ends.wait()
    wait_bytes(spread_ref.at[0, pl.ds(0, m // 2 - 1)], sr.at[0])
    pair = send(spread_ref.at[core], spread_ref.at[core], ss.at[1], sr.at[1], (z, chip * 2 + 1 - core))
    last.wait_send()
    first.wait_send()
    for copy in more:
        copy.wait_send()

    for r in range(2):
        for ch in range(CHUNKS):
            wait_bytes(xb.at[r, pl.ds(0, span)], zs.at[r, ch])
        for ch in range(CHUNKS - SENDING, CHUNKS):
            wait_bytes(stg.at[r, 0], ds.at[r, ch])
        for ch in range(CHUNKS - RING, CHUNKS):
            wait_bytes(ys.at[r, 0], ps.at[r, ch])
            wait_bytes(yo.at[r, 0], bs.at[r, ch])
    wait_bytes(spread_ref.at[0, pl.ds(0, m // 2 - 1)], ss.at[0])
    pair.wait_send()
    pair.wait_recv()


def experts_call(pick, weigh, choose, moe_in, resid, wg, wu, wd, slots):
    rows, tokens = pick.shape
    q, f = moe_in.shape[0], wg.shape[0]
    columns, groups = rows // slots, wg.shape[1] // q
    span = PER * slots
    dma = lambda *s: pltpu.SemaphoreType.DMA(s)
    big = lambda k: pltpu.VMEM((k, rows, q), BF)
    sending = pltpu.VMEM((2, SENDING, span, q), BF)
    ring = pltpu.VMEM((2, RING, span, q), BF)
    pair = dma(2, CHUNKS)
    return pl.pallas_call(
        functools.partial(expert_kernel, slots),
        out_shape=(
            jax.ShapeDtypeStruct((q, tokens), BF),
            jax.ShapeDtypeStruct((2, columns // 2, groups, 16, 256), BF),
        ),
        in_specs=[VMEM] * 5 + [ANY] * 3,
        out_specs=(VMEM, ANY),
        scratch_shapes=[
            pltpu.VMEM((q, tokens), BF),
            sending, big(4),
            pltpu.VMEM((groups * q, f), BF), pltpu.VMEM((groups * q, f), BF), pltpu.VMEM((groups, f, q), BF),
            pltpu.VMEM((2, 128, groups * q), BF),
            ring, ring, big(2), big(2),
            pltpu.VMEM((2, tokens, q), F32), pltpu.VMEM((tokens, q), BF), pltpu.VMEM((tokens, q), BF),
            pltpu.VMEM((groups, 16, 256), BF),
            dma(2), dma(2),
            pair, pair, pair, pair, pair, pair, pair, pair,
            dma(1), dma(2), dma(3), dma(3), dma(2), dma(2),
        ],
        compiler_params=pltpu.CompilerParams(
            collective_id=2, has_side_effects=True, vmem_limit_bytes=63 * 2**20
        ),
    )(pick, weigh, choose, moe_in, resid, wg, wu, wd)


def shards(
    hidden, segments, request_adapter, routes, expert_gates, attention_gain, joined_weight, sinks,
    attention_out_weight, joined_down_maps, joined_up_maps, output_down_maps, output_up_maps,
    expert_norm_gain, expert_gate_weight, expert_up_weight, expert_down_weight, closing_gain, vocabulary_weight,
):
    groups, columns = lax.axis_size("dp"), lax.axis_size("expert")
    z, c = lax.axis_index("dp"), lax.axis_index("expert")
    segment_row, adapter_row = segments[0], request_adapter[0]
    tokens, quarter = hidden.shape
    width = quarter * groups
    share = tokens // groups
    aux = jnp.concatenate(
        [routes[0].astype(BF), expert_gates[0], jnp.zeros((share, 128 - 2 * TOP), BF)], axis=1
    )
    hid4, aux4 = gather_z(hidden.T, aux)
    rows = hid4.reshape(width, tokens)

    wide = rows.astype(F32)
    mean_square = jnp.mean(wide * wide, axis=0, keepdims=True)
    normed = (wide * lax.rsqrt(mean_square + epsilon) * attention_gain[:, None]).astype(BF)
    ranks = joined_down_maps.shape[1]
    projected = dot_tn(joined_weight.reshape(width, -1), normed)
    low = dot_tn(joined_down_maps, normed).astype(BF)
    request_ids = jnp.arange(REQS, dtype=jnp.int32)
    hits = segment_row[None, :] == request_ids[:, None]
    adapter = jnp.sum(jnp.where(hits, adapter_row[:, None], 0), axis=0)
    mask = adapter[None, :] == (jnp.arange(ranks, dtype=jnp.int32) // ADAPTER_RANK)[:, None]
    low = jnp.where(mask, low, jnp.zeros_like(low))
    projected = projected + adapter_scale * dot_tn(joined_up_maps.reshape(ranks, -1), low)
    counter = jnp.arange(tokens, dtype=jnp.int32)
    starts = jnp.min(jnp.where(hits, counter[None, :], tokens), axis=1)
    positions = counter - jnp.sum(jnp.where(hits, starts[:, None], 0), axis=0)
    half = HEAD_SIZE // 2
    frequency = theta_base ** (-2.0 * jnp.arange(half, dtype=F32) / HEAD_SIZE)
    angles = frequency[:, None] * positions.astype(F32)[None, :]
    cosine, sine = jnp.cos(angles)[None], jnp.sin(angles)[None]
    projected = projected.reshape(QUERY_GROUP + 2, HEAD_SIZE, tokens)
    one, two = projected[: QUERY_GROUP + 1, :half], projected[: QUERY_GROUP + 1, half:]
    turned = jnp.concatenate([one * cosine - two * sine, two * cosine + one * sine], axis=1).astype(BF)
    queries, keys, values = turned[:QUERY_GROUP], turned[QUERY_GROUP], projected[QUERY_GROUP + 1].astype(BF)
    scores = jnp.einsum("ght,hs->gts", queries, keys, preferred_element_type=F32) * HEAD_SIZE ** (-0.5)
    allowed = (segment_row[:, None] == segment_row[None, :]) & (counter[None, :] <= counter[:, None])
    weights = jnp.where(allowed[None], jnp.exp(scores), 0.0)
    totals = jnp.sum(weights, axis=-1, keepdims=True) + jnp.exp(sinks).reshape(QUERY_GROUP, 1, 1)
    probs = (weights / totals).astype(BF)
    blended = jnp.einsum("hs,gts->ght", values, probs, preferred_element_type=F32)
    blended = blended.astype(BF).reshape(QUERY_GROUP * HEAD_SIZE, tokens)

    gain = lax.dynamic_slice_in_dim(expert_norm_gain, z * quarter, quarter)[:, None]
    resid, moe_in = out_project(
        blended, attention_out_weight.T, output_down_maps, hidden.T, mask.astype(F32), output_up_maps.T, gain
    )

    route_all = aux4[:, :, :TOP].reshape(tokens, TOP)
    gate_all = aux4[:, :, TOP : 2 * TOP].reshape(tokens, TOP)
    slots = CAP * groups
    targets = shifted(c, jnp.arange(columns, dtype=jnp.int32), 1).astype(BF)
    named = route_all[:, :, None] == targets[None, None, :]
    hit = jnp.any(named, axis=1)
    gate_of = jnp.sum(jnp.where(named, gate_all.astype(F32)[:, :, None], 0.0), axis=1)
    before = (counter[None, :] < counter[:, None]).astype(BF)
    rank = jnp.where(hit, dot(before, hit.astype(BF)), -1.0)
    slot_ids = jnp.arange(slots, dtype=F32)
    pick = (rank.T[:, None, :] == slot_ids[None, :, None]).astype(BF).reshape(columns * slots, tokens)
    weigh = jnp.where(rank[:, :, None] == slot_ids[None, None, :], gate_of[:, :, None], 0.0)
    weigh = weigh.astype(BF).reshape(tokens, columns * slots)
    last = jnp.max(jnp.where(hits, counter[None, :], -1), axis=1)
    choose = (counter[None, :] == last[:, None]).astype(BF)
    choose = jnp.concatenate([choose, choose, choose, jnp.zeros_like(choose)], axis=0)

    done, spread = experts_call(
        pick, weigh, choose, moe_in, resid, expert_gate_weight[0].T, expert_up_weight[0].T, expert_down_weight[0], slots
    )

    ends = spread[:, :, :, : 3 * REQS].reshape(2, columns // 2, groups, 3, REQS, 256)
    ends = jnp.transpose(ends, (1, 0, 4, 2, 3, 5)).reshape(columns * REQS, groups, 768)[:, :, :quarter]
    ends = ends.reshape(columns * REQS, width).astype(F32)
    mean_square = jnp.mean(ends * ends, axis=1, keepdims=True)
    ends = (ends * lax.rsqrt(mean_square + epsilon) * closing_gain).astype(BF)
    logits = dot(ends, vocabulary_weight)
    return done.T, logits


def solution(mesh):
    in_specs = (
        P("expert", "dp"),
        P("expert", None),
        P("expert", None),
        P("expert", "dp", None),
        P("expert", "dp", None),
        P(),
        P(None, "dp", None),
        P("dp"),
        P("dp", None),
        P(),
        P(None, "dp", None),
        P("dp", None),
        P(None, "dp"),
        P(),
        P("expert", None, "dp"),
        P("expert", None, "dp"),
        P("expert", "dp", None),
        P(),
        P(None, ("dp", "expert")),
    )
    out_specs = (P("expert", "dp"), P(None, ("dp", "expert")))
    return jax.shard_map(shards, mesh=mesh, in_specs=in_specs, out_specs=out_specs, check_vma=False)
```

time: 492 us -> 330 us (0.67); the launches traced: 483 us -> 329 us
  Pallas kernels: 345 us -> 279 us
  blocking collectives: 40.4 us -> 0 us
  local copies, waits for them, and re-layouts: 57.9 us -> 22.4 us
  matrix products: 23.4 us -> 13.9 us
    pallas_call x3 -> x2, Pallas kernels: 320 us -> 255 us  [the longest x1 218 us: experts_call(): pl.pallas_call(functools.partial(expert_kernel, slots), out_shape=(jax.Sh...]
    all_gather x1 -> x0, blocking collectives: 40.4 us -> none  [shards(): spread = lax.all_gather(chosen, ('dp', 'expert'), axis=0, tiled=True)]
    unnamed x38 -> x37, local copies, waits for them, and re-layouts: 27.5 us -> 7.66 us
    dot_general x6 -> x2, matrix products: 20.8 us -> 4.73 us  [dot(): return jnp.dot(a, b, preferred_element_type=F32)]
    convert_element_type x4 -> x1, local copies, waits for them, and re-layouts: 10.7 us -> 1.61 us  [shards(): ends = ends.reshape(columns * REQS, width).astype(F32)]
    dot_general x2 -> x4, matrix products: 2.61 us -> 9.21 us  [the longest x2 5.85 us: dot_tn(): lax.dot_general(a, b, (((0,), (0,)), ((), ())), preferred_element_type=F32)]
    another operation x1 -> x0, local copies, waits for them, and re-layouts: 6.51 us -> none  [shards(): expert_down_weight[0].reshape(-1, groups, quarter)]
    eq x0 -> x2, local copies, waits for them, and re-layouts: none -> 5.43 us  [shards(): rank[:, :, None] == slot_ids[None, None, :]]
where the time goes in v2:
time: 330 us; the launch traced here: 329 us
  Pallas kernels  279 us (85%)
  local copies, waits for them, and re-layouts  22.4 us (7%)
  matrix products  13.9 us (4%)
  other arithmetic  12.9 us (4%)
    pallas_call x1, Pallas kernels, experts_call(): pl.pallas_call(functools.partial(expert_kernel, slots), out_shape=(jax.Sh...  218 us
    pallas_call x1, Pallas kernels, out_project(): pl.pallas_call(out_kernel, out_shape=(jax.ShapeDtypeStruct((q, rows), BF)...  37.1 us
    pallas_call x1, Pallas kernels, gather_z(): pl.pallas_call(gather_kernel, out_shape=(jax.ShapeDtypeStruct((n,) + hidd...  24.5 us
    unnamed x37, local copies, waits for them, and re-layouts  7.66 us

profile of v2, /device:TPU:1, one launch (start us, length us, event | category | flops | bytes accessed | tf_op | source)
XLA Modules:
  0.0 329.4 jit_solution(5564902871301678774)
XLA Ops:
  0.6 0.8 copy.39
  1.5 0.8 copy.40
  2.5 1.0 copy-done.2
  3.5 24.5 %shard_map.194 = (bf16[4,720,384]{2,1,0:T(8,128)(2,1)S(1)}, bf16[4,96,128]{2,1,0:T(8,128)(2,1)S(1)}) custom-call(bf16[720,384]{1,0:T(8,128)(2,1)S(1)} %bitcast.79, bf16[96,128]{1,0:T(8,128)(2,1)S(1)} %maximum_maximum_fusion.a_ref), custom_call_target="tpu_custom_call" | custom-call | tf_op jit(solution)/shard_map/pallas_call | solution.py:109
  28.1 0.6 multiply_reduce_fusion
  28.6 0.8 mul.139
  29.4 0.6 multiply_convert_fusion
  30.0 1.5 copy-done.15
  31.5 3.0 fusion.3
  34.5 2.0 fusion.1
  36.8 2.8 fusion.10
  39.6 0.3 copy.46
  40.5 1.1 fusion.2
  41.8 2.2 fusion.11
  44.0 0.8 dynamic_slice.3
  45.1 1.8 copy-done.1
  46.9 37.1 %shard_map.195 = (bf16[720,384]{1,0:T(8,128)(2,1)S(1)}, bf16[720,384]{1,0:T(8,128)(2,1)S(1)}) custom-call(bf16[512,384]{1,0:T(8,128)(2,1)S(1)} %bitcast.81, bf16[2880,512]{1,0:T(8,128)(2,1)S(1)} %bitcast.78, bf16[512,128]{1,0:T(8,128)(2,1)S(1)} %copy-done.7, bf16[720,384]{1,0:T(8,128)(2,1)S(1)} %bitcast.80, f32[128,384]{1,0:T(8,128)S(1)} %compare_convert_fusion.mask_ref, ...), custom_call_target="tpu_custom_call" | custom-call | tf_op jit(solution)/shard_map/pallas_call | solution.py:181
  84.0 0.8 copy-done.4
  85.3 1.9 eq.137
  87.2 3.5 %copy.42 = f32[384,2048]{1,0:T(8,128)} copy(f32[384,2048]{0,1:T(8,128)} %bitcast.83) | data formatting | bytes 6291456 | tf_op jit(solution)/shard_map/eq | solution.py:560
  91.2 1.7 copy.44
  92.9 4.0 %select_convert_fusion.g_ref = bf16[384,2048]{1,0:T(8,128)(2,1)} fusion(bf16[384,2048]{1,0:T(8,128)(2,1)} %copy.44, f32[384,2048]{1,0:T(8,128)} %copy.42, f32[2048]{0:T(1024)S(1)} %eq.134), kind=kLoop, calls=%fused_computation.11 | loop fusion | flops 1572864 | bytes 6299648 | tf_op jit(solution)/shard_map/convert_element_type | solution.py:561
  97.0 1.5 fusion.5.d_ref
  98.6 0.7 maximum_maximum_fusion.1.e_ref
  99.3 217.6 %shard_map.196 = (bf16[720,384]{1,0:T(8,128)(2,1)}, bf16[2,16,4,16,256]{4,3,2,1,0:T(8,128)(2,1)}) custom-call(bf16[2048,384]{1,0:T(8,128)(2,1)} %fusion.5.d_ref, bf16[384,2048]{1,0:T(8,128)(2,1)} %select_convert_fusion.g_ref, bf16[16,384]{1,0:T(8,128)(2,1)} %maximum_maximum_fusion.1.e_ref, bf16[720,384]{1,0:T(8,128)(2,1)} %copy-done.5, ...), custom_call_target="tpu_custom_call" | custom-call | tf_op jit(solution)/shard_map/pallas_call | solution.py:470
  316.9 1.7 copy.50
  318.5 0.7 copy.51
  319.2 0.9 reshape.334
  320.3 1.6 copy.52
  322.2 1.8 fusion.8
  324.0 4.5 %fusion.46 = f32[128,800]{0,1:T(8,128)} fusion(bf16[2880,800]{0,1:T(8,128)(2,1)} %param.37, bf16[128,2880]{0,1:T(8,128)(2,1)S(1)} %fusion.8), kind=kOutput, calls=%fused_computation.109 | convolution fusion | flops 589824000 | bytes 5754880 | tf_op jit(solution)/shard_map/dot_general | solution.py:38
  328.6 0.8 copy.58
  (65 shorter events, 2.9 us)
Async XLA Ops:
  0.6 36.1 %copy-start = (bf16[2880,128]{1,0:T(8,128)(2,1)S(1)}, bf16[2880,128]{1,0:T(8,128)(2,1)}, u32[]{:S(2)}) copy-start(bf16[2880,128]{1,0:T(8,128)(2,1)} %param.28) | copy-start | bytes 2211844
  2.5 1.1 copy-start.2
  29.4 2.0 copy-start.15
  31.4 3.0 copy-start.11
  34.5 2.0 copy-start.13
  34.5 2.1 copy-start.14
  34.5 2.3 copy-start.10
  39.6 2.0 copy-start.8
  40.5 1.2 copy-start.16
  41.7 3.3 copy-start.3
  41.7 3.3 copy-start.6
  41.7 3.3 copy-start.7
  45.0 1.8 copy-start.1
  84.0 0.8 copy-start.4
  84.8 6.0 %copy-start.5 = (bf16[720,384]{1,0:T(8,128)(2,1)}, bf16[720,384]{1,0:T(8,128)(2,1)S(1)}, u32[]{:S(2)}) copy-start(bf16[720,384]{1,0:T(8,128)(2,1)S(1)} %get-tuple-element.10.mi_ref) | copy-start | bytes 1658884
  320.2 2.0 copy-start.12
  324.0 4.6 %copy-start.9 = (bf16[720,384]{1,0:T(8,128)(2,1)S(1)}, bf16[720,384]{1,0:T(8,128)(2,1)}, u32[]{:S(2)}) copy-start(bf16[720,384]{1,0:T(8,128)(2,1)} %get-tuple-element.12) | copy-start | bytes 1658884

commit v3 on v2

--- a/solution.py
+++ b/solution.py
@@ -15,11 +15,12 @@
 CAP = 16
 CHUNKS = 8
 PER = 4
-EARLY = 4
+EARLY = 3
 AHEAD = 2
+NEXT = 2
 BACK = 1
 ABSORB = 2
-SENDING = 5
+SENDING = 4
 RING = 3
 
 epsilon = 1e-05
@@ -126,8 +127,8 @@
 
 
 def out_kernel(
-    b_ref, wo_ref, odm_ref, hid_ref, mask_ref, oum_ref, gain_ref,
-    resid_ref, moe_ref,
+    b_ref, wo_ref, odm_ref, hid_ref, mask_ref, oum_ref, gain_ref, aux_ref, target_ref,
+    resid_ref, moe_ref, pick_ref, weigh_ref,
     low_snd, low_rcv, snd, rcv, st_snd, st_rcv, ss, rs,
 ):
     z, n, c, _ = place()
@@ -147,6 +148,24 @@
         copies.append(send(snd.at[o - 1], rcv.at[o - 1], ss.at[o + 2], rs.at[o + 2], (q, c)))
         copies.append(send(low_snd, low_rcv.at[o - 1], ss.at[o - 1], rs.at[o - 1], (q, c)))
     total = hid_ref[...].astype(F32) + part(z).astype(F32)
+
+    blocks, tokens = target_ref.shape[0], hid_ref.shape[1]
+    slots = pick_ref.shape[0] // blocks
+    aux = aux_ref[...]
+    hit = jnp.zeros((blocks, tokens), F32)
+    gate = jnp.zeros((blocks, tokens), F32)
+    for k in range(TOP):
+        same = aux[k : k + 1] == target_ref[:, :1]
+        hit = jnp.where(same, 1.0, hit)
+        gate = jnp.where(same, aux[TOP + k : TOP + k + 1], gate)
+    before = lax.broadcasted_iota(jnp.int32, (tokens, tokens), 0) < lax.broadcasted_iota(jnp.int32, (tokens, tokens), 1)
+    rank = jnp.where(hit > 0.5, dot(hit.astype(BF), before.astype(F32).astype(BF)), -1.0)
+    ids = lax.broadcasted_iota(jnp.int32, (slots, tokens), 0).astype(F32)
+    for j in range(blocks):
+        here = ids == rank[j : j + 1]
+        pick_ref[j * slots : (j + 1) * slots] = jnp.where(here, 1.0, 0.0).astype(BF)
+        weigh_ref[j * slots : (j + 1) * slots] = jnp.where(here, gate[j : j + 1], 0.0).astype(BF)
+
     for copy in copies[1::2]:
         copy.wait_recv()
     low_sum = low.astype(F32)
@@ -175,14 +194,15 @@
         copy.wait_send()
 
 
-def out_project(blended, wo, odm, hidden, mask, oum, gain):
+def out_project(blended, wo, odm, hidden, mask, oum, gain, aux, targets, slots):
     q, rows = hidden.shape
+    table = jax.ShapeDtypeStruct((targets.shape[0] * slots, rows), BF)
     n = 3
     return pl.pallas_call(
         out_kernel,
-        out_shape=(jax.ShapeDtypeStruct((q, rows), BF), jax.ShapeDtypeStruct((q, rows), BF)),
-        in_specs=[VMEM] * 7,
-        out_specs=(VMEM, VMEM),
+        out_shape=(jax.ShapeDtypeStruct((q, rows), BF), jax.ShapeDtypeStruct((q, rows), BF), table, table),
+        in_specs=[VMEM] * 9,
+        out_specs=(VMEM,) * 4,
         scratch_shapes=[
             pltpu.VMEM(mask.shape, BF),
             pltpu.VMEM((n,) + mask.shape, BF),
@@ -196,7 +216,7 @@
         compiler_params=pltpu.CompilerParams(
             collective_id=1, has_side_effects=True, vmem_limit_bytes=48 * 2**20
         ),
-    )(blended, wo, odm, hidden, mask, oum, gain)
+    )(blended, wo, odm, hidden, mask, oum, gain, aux, targets)
 
 
 def shift_of(j):
@@ -213,7 +233,7 @@
 def expert_kernel(
     slots, d_ref, g_ref, e_ref, mi_ref, resid_ref, wg_hbm, wu_hbm, wd_hbm,
     out_ref, spread_ref,
-    mi_nb, stg, xb, wg, wu, wd, raw, yo, ys, yr, ans, macc, m1s, m1r, pk,
+    mi_nb, stg, xb, wg, wu, wd, raw, yo, ys, yr, ans, macc, m1s, m1r, e1s, e1r, pk,
     w_sem, mi_sem, ds, dr, zs, zr, ps, pr, bs, br, own_sem, m_sem, ks, kr, ss, sr,
 ):
     z, n, c, m = place()
@@ -289,11 +309,10 @@
         def _():
             wait_bytes(buffer.at[r, chunk(ch)], sem.at[r, ch])
 
-    def forward(ch):
-        came_in_plane(xb, dr, 0, ch)
-        send(xb.at[0, chunk(ch)], xb.at[2, chunk(ch)], zs.at[0, ch], zr.at[0, ch], (away(ch), c))
-        came_in_plane(xb, dr, 1, ch)
-        send(xb.at[1, chunk(ch)], xb.at[3, chunk(ch)], zs.at[1, ch], zr.at[1, ch], (near(ch), c))
+    def forward(ch, r):
+        came_in_plane(xb, dr, r, ch)
+        there = (away(ch), near(ch))[r]
+        send(xb.at[r, chunk(ch)], xb.at[r + 2, chunk(ch)], zs.at[r, ch], zr.at[r, ch], (there, c))
 
     def experts(ch):
         slot = lax.rem(ch, RING)
@@ -342,7 +361,7 @@
     def absorb(ch):
         for r in (1, 0):
             came_in_plane(ans, br, r, ch)
-            macc[r] += dot(g_ref[:, chunk(ch)], ans[r, chunk(ch)])
+            macc[r] += dot_tn(g_ref[chunk(ch)], ans[r, chunk(ch)])
 
     steps = [(w, h0, min(128, q - h0)) for w in range(3) for h0 in range(0, q, 128)]
 
@@ -354,18 +373,37 @@
 
     fetch(0).start()
 
-    @pl.loop(0, EARLY)
+    head = 2
+
+    @pl.loop(0, head)
     def _(ch):
         dispatch(ch, 0)
 
     macc[...] = jnp.zeros_like(macc)
     first.wait_recv()
 
-    @pl.loop(0, EARLY)
+    @pl.loop(0, head)
     def _(ch):
         dispatch(ch, 1)
 
+    @pl.loop(head, EARLY)
+    def _(ch):
+        dispatch(ch, 0)
+        dispatch(ch, 1)
+
     for i, (w, h0, hs) in enumerate(steps):
+        if i == len(steps) // 3:
+
+            @pl.loop(0, AHEAD)
+            def _(ch):
+                forward(ch, 0)
+
+        if i == 2 * len(steps) // 3:
+
+            @pl.loop(0, NEXT)
+            def _(ch):
+                forward(ch, 1)
+
         if i + 1 < len(steps):
             fetch(i + 1).start()
         fetch(i).wait()
@@ -385,41 +423,45 @@
             for f in range(4):
                 wd[f, h0 : h0 + hs, :] = raw[i % 2, :hs, f * q : (f + 1) * q]
 
-    @pl.loop(0, CHUNKS + AHEAD + BACK)
+    @pl.loop(0, CHUNKS + BACK)
     def _(t):
-        @pl.when(t < CHUNKS)
-        def _():
-            forward(t)
+        @pl.when(t + AHEAD < CHUNKS)
+        def _():
+            forward(t + AHEAD, 0)
+
+        @pl.when(t + NEXT < CHUNKS)
+        def _():
+            forward(t + NEXT, 1)
 
         @pl.when(t + EARLY < CHUNKS)
         def _():
             dispatch(t + EARLY, 0)
             dispatch(t + EARLY, 1)
 
-        @pl.when((t >= AHEAD) & (t < CHUNKS + AHEAD))
-        def _():
-            experts(t - AHEAD)
-
-        @pl.when(t >= AHEAD + BACK)
-        def _():
-            give_back(t - AHEAD - BACK)
-
-        @pl.when(t >= AHEAD + BACK + ABSORB)
-        def _():
-            absorb(t - AHEAD - BACK - ABSORB)
+        @pl.when(t < CHUNKS)
+        def _():
+            experts(t)
+
+        @pl.when(t >= BACK)
+        def _():
+            give_back(t - BACK)
+
+        @pl.when(t >= BACK + ABSORB)
+        def _():
+            absorb(t - BACK - ABSORB)
 
     @pl.loop(CHUNKS - ABSORB, CHUNKS)
     def _(ch):
         absorb(ch)
 
     m1s[...] = macc[1].astype(BF)
+    e1s[...] = dot(e_ref[...], m1s[...]).astype(BF)
+    hasty = send(e1s, e1r, m_sem.at[2], m_sem.at[3], (away(0), c))
     last = send(m1s, m1r, m_sem.at[0], m_sem.at[1], (away(0), c))
-    last.wait_recv()
-    moe = (macc[0] + m1r[...].astype(F32)).astype(BF)
-    done = (resid_ref[...].astype(F32) + moe.T.astype(F32)).astype(BF)
-    out_ref[...] = done
-
-    ends = dot_nt(e_ref[...], done)
+    ends = jnp.dot(e_ref[...].astype(F32), macc[0], preferred_element_type=F32, precision=lax.Precision.HIGHEST)
+    kept = dot_nt(e_ref[...], resid_ref[...])
+    hasty.wait_recv()
+    ends = kept + (ends + e1r[...].astype(F32)).astype(BF).astype(F32)
     ends = jnp.concatenate([ends, jnp.zeros((ends.shape[0], 768 - q), F32)], axis=1)
     piece = lax.broadcasted_iota(jnp.int32, (ends.shape[0], 256), 0) // REQS
     packed = jnp.where(piece == 0, ends[:, :256], jnp.where(piece == 1, ends[:, 256:512], ends[:, 512:]))
@@ -436,10 +478,14 @@
         there = (((chip // 4 + j // 4) % 4) * 4 + (chip + j) % 4) * 2 + core
         send(pk, spread_ref.at[core, chip], ss.at[0], sr.at[0], (z, there))
 
+    last.wait_recv()
+    moe = (macc[0] + m1r[...].astype(F32)).astype(BF)
+    out_ref[...] = (resid_ref[...].astype(F32) + moe.T.astype(F32)).astype(BF)
     own_ends.wait()
     wait_bytes(spread_ref.at[0, pl.ds(0, m // 2 - 1)], sr.at[0])
     pair = send(spread_ref.at[core], spread_ref.at[core], ss.at[1], sr.at[1], (z, chip * 2 + 1 - core))
     last.wait_send()
+    hasty.wait_send()
     first.wait_send()
     for copy in more:
         copy.wait_send()
@@ -482,10 +528,11 @@
             pltpu.VMEM((2, 128, groups * q), BF),
             ring, ring, big(2), big(2),
             pltpu.VMEM((2, tokens, q), F32), pltpu.VMEM((tokens, q), BF), pltpu.VMEM((tokens, q), BF),
+            pltpu.VMEM((16, q), BF), pltpu.VMEM((16, q), BF),
             pltpu.VMEM((groups, 16, 256), BF),
             dma(2), dma(2),
             pair, pair, pair, pair, pair, pair, pair, pair,
-            dma(1), dma(2), dma(3), dma(3), dma(2), dma(2),
+            dma(1), dma(4), dma(3), dma(3), dma(2), dma(2),
         ],
         compiler_params=pltpu.CompilerParams(
             collective_id=2, has_side_effects=True, vmem_limit_bytes=63 * 2**20
@@ -504,9 +551,8 @@
     tokens, quarter = hidden.shape
     width = quarter * groups
     share = tokens // groups
-    aux = jnp.concatenate(
-        [routes[0].astype(BF), expert_gates[0], jnp.zeros((share, 128 - 2 * TOP), BF)], axis=1
-    )
+    aux = jnp.concatenate([routes[0].T.astype(BF), expert_gates[0].T], axis=0)
+    aux = jnp.pad(aux, ((0, 16 - 2 * TOP), (0, 128 - share)))
     hid4, aux4 = gather_z(hidden.T, aux)
     rows = hid4.reshape(width, tokens)
 
@@ -542,23 +588,14 @@
     blended = blended.astype(BF).reshape(QUERY_GROUP * HEAD_SIZE, tokens)
 
     gain = lax.dynamic_slice_in_dim(expert_norm_gain, z * quarter, quarter)[:, None]
-    resid, moe_in = out_project(
-        blended, attention_out_weight.T, output_down_maps, hidden.T, mask.astype(F32), output_up_maps.T, gain
+    slots = CAP * groups
+    aux = jnp.transpose(aux4[:, :, :share], (1, 0, 2)).reshape(16, tokens).astype(F32)
+    targets = shifted(c, jnp.arange(columns, dtype=jnp.int32), 1).astype(F32)
+    targets = jnp.broadcast_to(targets[:, None], (columns, 128))
+    resid, moe_in, pick, weigh = out_project(
+        blended, attention_out_weight.T, output_down_maps, hidden.T, mask.astype(F32), output_up_maps.T, gain,
+        aux, targets, slots
     )
-
-    route_all = aux4[:, :, :TOP].reshape(tokens, TOP)
-    gate_all = aux4[:, :, TOP : 2 * TOP].reshape(tokens, TOP)
-    slots = CAP * groups
-    targets = shifted(c, jnp.arange(columns, dtype=jnp.int32), 1).astype(BF)
-    named = route_all[:, :, None] == targets[None, None, :]
-    hit = jnp.any(named, axis=1)
-    gate_of = jnp.sum(jnp.where(named, gate_all.astype(F32)[:, :, None], 0.0), axis=1)
-    before = (counter[None, :] < counter[:, None]).astype(BF)
-    rank = jnp.where(hit, dot(before, hit.astype(BF)), -1.0)
-    slot_ids = jnp.arange(slots, dtype=F32)
-    pick = (rank.T[:, None, :] == slot_ids[None, :, None]).astype(BF).reshape(columns * slots, tokens)
-    weigh = jnp.where(rank[:, :, None] == slot_ids[None, None, :], gate_of[:, :, None], 0.0)
-    weigh = weigh.astype(BF).reshape(tokens, columns * slots)
     last = jnp.max(jnp.where(hits, counter[None, :], -1), axis=1)
     choose = (counter[None, :] == last[:, None]).astype(BF)
     choose = jnp.concatenate([choose, choose, choose, jnp.zeros_like(choose)], axis=0)

time: 330 us -> 306 us (0.927)
  Pallas kernels: 279 us -> 265 us
  local copies, waits for them, and re-layouts: 22.4 us -> 17.1 us
  other arithmetic: 12.9 us -> 7.77 us
    pallas_call x1, Pallas kernels: 218 us -> 202 us  [experts_call(): pl.pallas_call(functools.partial(expert_kernel, slots), out_shape=(jax.Sh...]
    eq x5 -> x0, local copies, waits for them, and re-layouts: 5.6 us -> none  [the longest x2 5.43 us: shards(): rank[:, :, None] == slot_ids[None, None, :]]
    convert_element_type x5 -> x3, other arithmetic: 5.57 us -> 0.72 us  [the longest x1 0.69 us: shards(): aux = jnp.concatenate([routes[0].T.astype(BF), expert_gates[0].T], axis=0)]
    unnamed x37 -> x35, local copies, waits for them, and re-layouts: 7.66 us -> 8.72 us
where the time goes in v3:
time: 306 us
  Pallas kernels  265 us (87%)
  local copies, waits for them, and re-layouts  17.1 us (6%)
  matrix products  14.7 us (5%)
  other arithmetic  7.77 us (3%)
    pallas_call x1, Pallas kernels, experts_call(): pl.pallas_call(functools.partial(expert_kernel, slots), out_shape=(jax.Sh...  202 us
    pallas_call x1, Pallas kernels, out_project(): pl.pallas_call(out_kernel, out_shape=(jax.ShapeDtypeStruct((q, rows), BF)...  39 us
    pallas_call x1, Pallas kernels, gather_z(): pl.pallas_call(gather_kernel, out_shape=(jax.ShapeDtypeStruct((n,) + hidd...  23.6 us
    unnamed x35, local copies, waits for them, and re-layouts  8.72 us

profile of v3, /device:TPU:1, one launch (start us, length us, event | category | flops | bytes accessed | tf_op | source)
XLA Modules:
  0.0 305.6 jit_solution(14518645356925936536)
XLA Ops:
  0.6 0.8 reduce.2
  1.5 0.8 mul.137
  2.3 0.7 convert_bitcast_fusion.1
  3.0 0.7 fusion.33.a_ref
  3.7 1.0 copy-done.1
  4.8 23.6 %shard_map.194 = (bf16[4,720,384]{2,1,0:T(8,128)(2,1)S(1)}, bf16[4,16,128]{2,1,0:T(8,128)(2,1)S(1)}) custom-call(bf16[720,384]{1,0:T(8,128)(2,1)S(1)} %bitcast.72, bf16[16,128]{1,0:T(8,128)(2,1)S(1)} %fusion.33.a_ref), custom_call_target="tpu_custom_call" | custom-call | tf_op jit(solution)/shard_map/pallas_call | solution.py:110
  28.4 0.6 multiply_reduce_fusion
  29.0 0.6 multiply_convert_fusion
  29.6 3.0 fusion.3
  32.6 0.6 fusion.1
  33.5 3.1 %fusion.9 = f32[640,384]{0,1:T(8,128)} fusion(f32[384,640]{1,0:T(8,128)} %fusion.3, bf16[2880,384]{1,0:T(8,128)(2,1)S(1)} %fusion.1, bf16[2880,128]{1,0:T(8,128)(2,1)S(1)} %copy-done, bf16[128,1,640]{2,0,1:T(8,128)(2,1)S(1)} %copy-done.11, s32[384]{0:T(512)S(1)} %get-tuple-element.20, s32[128]{0:T(128)S(1)} %and_select_fusion.8), kind=kOutput, calls=%fused_computation.17 | convolution fusion | flops 346669056 | bytes 5081088 | tf_op jit(solution)/shard_map/dot_general | solution.py:47
  36.6 1.5 copy.35
  38.6 1.1 fusion.2
  39.8 3.0 fusion.10
  42.8 0.8 dynamic_slice.3
  44.0 1.0 copy-done.7
  45.0 0.9 copy-done.8
  45.9 0.9 copy-done.9
  46.8 39.0 %shard_map.195 = (bf16[720,384]{1,0:T(8,128)(2,1)S(1)}, bf16[720,384]{1,0:T(8,128)(2,1)S(1)}, bf16[2048,384]{1,0:T(8,128)(2,1)S(1)}, bf16[2048,384]{1,0:T(8,128)(2,1)S(1)}) custom-call(bf16[512,384]{1,0:T(8,128)(2,1)S(1)} %bitcast.74, bf16[2880,512]{1,0:T(8,128)(2,1)} %bitcast.81, bf16[512,128]{1,0:T(8,128)(2,1)S(1)} %copy-done.9, ...), custom_call_target="tpu_custom_call" | custom-call | tf_op jit(solution)/shard_map/pallas_call | solution.py:201
  85.8 1.1 copy-done.3
  87.0 1.2 copy-done.4
  88.1 0.8 copy-done.5
  89.0 0.8 copy-done.6
  89.9 0.7 maximum_maximum_fusion.e_ref
  90.6 202.5 %shard_map.196 = (bf16[720,384]{1,0:T(8,128)(2,1)}, bf16[2,16,4,16,256]{4,3,2,1,0:T(8,128)(2,1)}) custom-call(bf16[2048,384]{1,0:T(8,128)(2,1)} %copy-done.3, bf16[2048,384]{1,0:T(8,128)(2,1)} %copy-done.4, bf16[16,384]{1,0:T(8,128)(2,1)} %maximum_maximum_fusion.e_ref, bf16[720,384]{1,0:T(8,128)(2,1)} %copy-done.6, bf16[720,384]{1,0:T(8,128)(2,1)} %copy-done.5, ...), custom_call_target="tpu_custom_call" | custom-call | tf_op jit(solution)/shard_map/pallas_call | solution.py:516
  293.0 1.7 copy.40
  294.7 0.7 copy.41
  295.4 0.9 reshape.318
  296.5 1.6 copy.42
  298.4 1.8 fusion.7
  300.2 4.5 %fusion.49 = f32[128,800]{0,1:T(8,128)} fusion(bf16[2880,800]{0,1:T(8,128)(2,1)} %param.37, bf16[128,2880]{0,1:T(8,128)(2,1)S(1)} %fusion.7), kind=kOutput, calls=%fused_computation.107 | convolution fusion | flops 589824000 | bytes 5754880 | tf_op jit(solution)/shard_map/dot_general | solution.py:39
  304.8 0.8 copy.48
  (50 shorter events, 2.0 us)
Async XLA Ops:
  0.6 32.8 %copy-start = (bf16[2880,128]{1,0:T(8,128)(2,1)S(1)}, bf16[2880,128]{1,0:T(8,128)(2,1)}, u32[]{:S(2)}) copy-start(bf16[2880,128]{1,0:T(8,128)(2,1)} %param.28) | copy-start | bytes 2211844
  3.7 1.1 copy-start.1
  4.8 24.8 %copy-start.15 = (bf16[2880,1,640]{2,0,1:T(8,128)(2,1)S(1)}, bf16[2880,1,640]{2,0,1:T(8,128)(2,1)}, u32[]{:S(2)}) copy-start(bf16[2880,1,640]{2,0,1:T(8,128)(2,1)} %param.25) | copy-start | bytes 11059204
  29.5 3.0 copy-start.12
  32.6 0.7 copy-start.14
  32.6 0.9 copy-start.11
  38.5 1.2 copy-start.16
  39.8 4.2 %copy-start.2 = (bf16[384,720]{0,1:T(8,128)(2,1)S(1)}, bf16[384,720]{0,1:T(8,128)(2,1)}, u32[]{:S(2)}) copy-start(bf16[384,720]{0,1:T(8,128)(2,1)} %param.19) | copy-start | bytes 1658884
  44.0 1.0 copy-start.7
  45.0 0.9 copy-start.8
  45.9 0.9 copy-start.9
  85.8 1.2 copy-start.3
  87.0 1.2 copy-start.4
  88.1 0.8 copy-start.5
  88.9 0.8 copy-start.6
  295.4 3.0 copy-start.13
  300.2 4.6 %copy-start.10 = (bf16[720,384]{1,0:T(8,128)(2,1)S(1)}, bf16[720,384]{1,0:T(8,128)(2,1)}, u32[]{:S(2)}) copy-start(bf16[720,384]{1,0:T(8,128)(2,1)} %get-tuple-element.16) | copy-start | bytes 1658884

commit v4 on v3

--- a/solution.py
+++ b/solution.py
@@ -127,27 +127,58 @@
 
 
 def out_kernel(
-    b_ref, wo_ref, odm_ref, hid_ref, mask_ref, oum_ref, gain_ref, aux_ref, target_ref,
+    b_ref, wo_hbm, odm_hbm, hid_hbm, mask_ref, oum_hbm, gain_ref, aux_ref, target_ref,
     resid_ref, moe_ref, pick_ref, weigh_ref,
-    low_snd, low_rcv, snd, rcv, st_snd, st_rcv, ss, rs,
+    wo_ref, odm_ref, hid_ref, oum_ref, low_snd, low_rcv, far, passed, snd, rcv, st_snd, st_rcv, fetch, ss, rs,
 ):
     z, n, c, _ = place()
+    loads = [
+        pltpu.make_async_copy(src, dst, fetch.at[i])
+        for i, (src, dst) in enumerate(
+            ((wo_hbm, wo_ref), (odm_hbm, odm_ref), (hid_hbm, hid_ref), (oum_hbm, oum_ref))
+        )
+    ]
+    for load in loads:
+        load.start()
     quarter = hid_ref.shape[0]
+    half = quarter // 32 * 16
+    lo, hi = pl.ds(0, half), pl.ds(half, quarter - half)
+    zu, zf, zd = lax.rem(z + 1, n), lax.rem(z + 2, n), lax.rem(z + 3, n)
+    up, down = (zu, c), (zd, c)
     blended = b_ref[...]
 
     def part(q):
-        return dot(wo_ref[pl.ds(pl.multiple_of(q * quarter, 16), quarter)], blended).astype(BF)
-
+        return dot(wo_ref[pl.ds(pl.multiple_of(q * quarter, 16), quarter)], blended)
+
+    greet_z((1, 2, 3))
+    loads[0].wait()
+    far[...] = part(zf).astype(BF)
+    relays = [
+        send(far.at[lo], passed.at[lo], ss.at[3], rs.at[3], up),
+        send(far.at[hi], passed.at[hi], ss.at[4], rs.at[4], down),
+    ]
+    above, below = part(zu), part(zd)
+    snd[0, half:] = above[half:].astype(BF)
+    snd[1, :half] = below[:half].astype(BF)
+    shares = [
+        send(snd.at[0, hi], rcv.at[0, hi], ss.at[5], rs.at[5], up),
+        send(snd.at[1, lo], rcv.at[1, lo], ss.at[6], rs.at[6], down),
+    ]
+    loads[1].wait()
     low = dot_tn(odm_ref[...], blended).astype(BF)
     low_snd[...] = low
-    greet_z((1, 2, 3))
-    copies = []
-    for o in (2, 1, 3):
-        q = lax.rem(z + o, n)
-        snd[o - 1] = part(q)
-        copies.append(send(snd.at[o - 1], rcv.at[o - 1], ss.at[o + 2], rs.at[o + 2], (q, c)))
-        copies.append(send(low_snd, low_rcv.at[o - 1], ss.at[o - 1], rs.at[o - 1], (q, c)))
-    total = hid_ref[...].astype(F32) + part(z).astype(F32)
+    lows = [
+        send(low_snd, low_rcv.at[o - 1], ss.at[o - 1], rs.at[o - 1], (lax.rem(z + o, n), c)) for o in (2, 1, 3)
+    ]
+    relays[0].wait_recv()
+    snd[0, :half] = (above[:half] + passed[:half].astype(F32)).astype(BF)
+    shares.append(send(snd.at[0, lo], rcv.at[0, lo], ss.at[7], rs.at[7], up))
+    relays[1].wait_recv()
+    snd[1, half:] = (below[half:] + passed[half:].astype(F32)).astype(BF)
+    shares.append(send(snd.at[1, hi], rcv.at[1, hi], ss.at[8], rs.at[8], down))
+    for load in loads[2:]:
+        load.wait()
+    total = hid_ref[...].astype(F32) + part(z)
 
     blocks, tokens = target_ref.shape[0], hid_ref.shape[1]
     slots = pick_ref.shape[0] // blocks
@@ -166,17 +197,16 @@
         pick_ref[j * slots : (j + 1) * slots] = jnp.where(here, 1.0, 0.0).astype(BF)
         weigh_ref[j * slots : (j + 1) * slots] = jnp.where(here, gate[j : j + 1], 0.0).astype(BF)
 
-    for copy in copies[1::2]:
+    for copy in lows:
         copy.wait_recv()
     low_sum = low.astype(F32)
     for k in range(3):
         low_sum = low_sum + low_rcv[k].astype(F32)
     picked = (low_sum * mask_ref[...]).astype(BF)
     total = total + adapter_scale * dot(oum_ref[...], picked)
-    for copy in copies[0::2]:
+    for copy in shares:
         copy.wait_recv()
-    for k in range(3):
-        total = total + rcv[k].astype(F32)
+    total = total + rcv[0].astype(F32) + rcv[1].astype(F32)
     resid = total.astype(BF)
     resid_ref[...] = resid
     wide = resid.astype(F32)
@@ -184,13 +214,13 @@
     st_snd[...] = jnp.broadcast_to(sums, st_snd.shape)
     more = []
     for o in (2, 1, 3):
-        more.append(send(st_snd, st_rcv.at[o - 1], ss.at[o + 5], rs.at[o + 5], (lax.rem(z + o, n), c)))
+        more.append(send(st_snd, st_rcv.at[o - 1], ss.at[o + 8], rs.at[o + 8], (lax.rem(z + o, n), c)))
     for copy in more:
         copy.wait_recv()
     every = st_snd[...] + st_rcv[0] + st_rcv[1] + st_rcv[2]
     scale = lax.rsqrt(every / (4.0 * quarter) + epsilon)
     moe_ref[...] = (wide * scale[:1] * gain_ref[...]).astype(BF)
-    for copy in copies + more:
+    for copy in relays + shares + lows + more:
         copy.wait_send()
 
 
@@ -201,17 +231,24 @@
     return pl.pallas_call(
         out_kernel,
         out_shape=(jax.ShapeDtypeStruct((q, rows), BF), jax.ShapeDtypeStruct((q, rows), BF), table, table),
-        in_specs=[VMEM] * 9,
+        in_specs=[VMEM, ANY, ANY, ANY, VMEM, ANY, VMEM, VMEM, VMEM],
         out_specs=(VMEM,) * 4,
         scratch_shapes=[
+            pltpu.VMEM(wo.shape, BF),
+            pltpu.VMEM(odm.shape, BF),
+            pltpu.VMEM(hidden.shape, BF),
+            pltpu.VMEM(oum.shape, BF),
             pltpu.VMEM(mask.shape, BF),
             pltpu.VMEM((n,) + mask.shape, BF),
-            pltpu.VMEM((n, q, rows), BF),
-            pltpu.VMEM((n, q, rows), BF),
+            pltpu.VMEM((q, rows), BF),
+            pltpu.VMEM((q, rows), BF),
+            pltpu.VMEM((2, q, rows), BF),
+            pltpu.VMEM((2, q, rows), BF),
             pltpu.VMEM((8, rows), F32),
             pltpu.VMEM((n, 8, rows), F32),
-            pltpu.SemaphoreType.DMA((9,)),
-            pltpu.SemaphoreType.DMA((9,)),
+            pltpu.SemaphoreType.DMA((4,)),
+            pltpu.SemaphoreType.DMA((12,)),
+            pltpu.SemaphoreType.DMA((12,)),
         ],
         compiler_params=pltpu.CompilerParams(
             collective_id=1, has_side_effects=True, vmem_limit_bytes=48 * 2**20
@@ -231,12 +268,18 @@
 
 
 def expert_kernel(
-    slots, d_ref, g_ref, e_ref, mi_ref, resid_ref, wg_hbm, wu_hbm, wd_hbm,
+    slots, d_hbm, g_hbm, e_ref, mi_hbm, resid_hbm, wg_hbm, wu_hbm, wd_hbm,
     out_ref, spread_ref,
-    mi_nb, stg, xb, wg, wu, wd, raw, yo, ys, yr, ans, macc, m1s, m1r, e1s, e1r, pk,
+    d_ref, g_ref, mi_ref, resid_ref, fetched, mi_nb, stg, xb, wg, wu, wd, raw, yo, ys, yr, ans, macc, m1s, m1r, e1s, e1r, pk,
     w_sem, mi_sem, ds, dr, zs, zr, ps, pr, bs, br, own_sem, m_sem, ks, kr, ss, sr,
 ):
     z, n, c, m = place()
+    loads = [
+        pltpu.make_async_copy(src, dst, fetched.at[i])
+        for i, (src, dst) in enumerate(((mi_hbm, mi_ref), (d_hbm, d_ref), (g_hbm, g_ref), (resid_hbm, resid_ref)))
+    ]
+    for load in loads:
+        load.start()
     span = PER * slots
     q = mi_ref.shape[0]
 
@@ -261,6 +304,7 @@
     for o in (1, 2, 3):
         pl.semaphore_signal(barrier, inc=1, device_id=(lax.rem(z + o, n), c), device_id_type=MESH)
     pl.semaphore_wait(barrier, m + 2)
+    loads[0].wait()
     first = send(mi_ref, mi_nb, mi_sem.at[0], mi_sem.at[1], (near(0), c))
 
     def block(j):
@@ -373,6 +417,7 @@
 
     fetch(0).start()
 
+    loads[1].wait()
     head = 2
 
     @pl.loop(0, head)
@@ -380,6 +425,8 @@
         dispatch(ch, 0)
 
     macc[...] = jnp.zeros_like(macc)
+    loads[2].wait()
+    loads[3].wait()
     first.wait_recv()
 
     @pl.loop(0, head)
@@ -519,9 +566,11 @@
             jax.ShapeDtypeStruct((q, tokens), BF),
             jax.ShapeDtypeStruct((2, columns // 2, groups, 16, 256), BF),
         ),
-        in_specs=[VMEM] * 5 + [ANY] * 3,
+        in_specs=[ANY, ANY, VMEM] + [ANY] * 5,
         out_specs=(VMEM, ANY),
         scratch_shapes=[
+            pltpu.VMEM(pick.shape, BF), pltpu.VMEM(weigh.shape, BF),
+            pltpu.VMEM((q, tokens), BF), pltpu.VMEM((q, tokens), BF), dma(4),
             pltpu.VMEM((q, tokens), BF),
             sending, big(4),
             pltpu.VMEM((groups * q, f), BF), pltpu.VMEM((groups * q, f), BF), pltpu.VMEM((groups, f, q), BF),
@@ -538,6 +587,50 @@
             collective_id=2, has_side_effects=True, vmem_limit_bytes=63 * 2**20
         ),
     )(pick, weigh, choose, moe_in, resid, wg, wu, wd)
+
+
+def head_kernel(spread_ref, gain_ref, vocab_hbm, out_ref, vocab_ref, sem):
+    entries = out_ref.shape[0]
+    parts = entries // 160
+    loads = [
+        pltpu.make_async_copy(vocab_hbm.at[pl.ds(i * 160, 160)], vocab_ref.at[pl.ds(i * 160, 160)], sem.at[i])
+        for i in range(parts)
+    ]
+    for load in loads:
+        load.start()
+    holders, groups, packed, lanes = spread_ref.shape
+    rows = out_ref.shape[1]
+    width = vocab_ref.shape[1]
+    quarter = width // groups
+    to = lax.broadcasted_iota(jnp.int32, (rows, holders * packed), 0)
+    at = lax.broadcasted_iota(jnp.int32, (rows, holders * packed), 1)
+    start = (((to >> 2) & 1) * (holders // 2) + (to >> 3)) * packed + (to & 3)
+    select = [jnp.where(at == start + REQS * i, 1.0, 0.0).astype(BF) for i in range(3)]
+    pieces = []
+    squares = jnp.zeros((rows, 1), F32)
+    for f in range(groups):
+        block = spread_ref[:, f].reshape(holders * packed, lanes)
+        for i in range(3):
+            piece = dot(select[i], block)
+            squares = squares + jnp.sum(piece * piece, axis=1, keepdims=True)
+            pieces.append(piece[:, : min(lanes, quarter - i * lanes)])
+    scale = lax.rsqrt(squares / width + epsilon)
+    ends = (jnp.concatenate(pieces, axis=1) * scale * gain_ref[...]).astype(BF)
+    for i in range(parts):
+        loads[i].wait()
+        out_ref[i * 160 : (i + 1) * 160] = dot_nt(vocab_ref[i * 160 : (i + 1) * 160], ends)
+
+
+def head(spread, gain, vocab):
+    entries = vocab.shape[0]
+    return pl.pallas_call(
+        head_kernel,
+        out_shape=jax.ShapeDtypeStruct((entries, spread.shape[0] * REQS), F32),
+        in_specs=[VMEM, VMEM, ANY],
+        out_specs=VMEM,
+        scratch_shapes=[pltpu.VMEM(vocab.shape, BF), pltpu.SemaphoreType.DMA((entries // 160,))],
+        compiler_params=pltpu.CompilerParams(vmem_limit_bytes=32 * 2**20),
+    )(spread, gain, vocab)
 
 
 def shards(
@@ -604,13 +697,8 @@
         pick, weigh, choose, moe_in, resid, expert_gate_weight[0].T, expert_up_weight[0].T, expert_down_weight[0], slots
     )
 
-    ends = spread[:, :, :, : 3 * REQS].reshape(2, columns // 2, groups, 3, REQS, 256)
-    ends = jnp.transpose(ends, (1, 0, 4, 2, 3, 5)).reshape(columns * REQS, groups, 768)[:, :, :quarter]
-    ends = ends.reshape(columns * REQS, width).astype(F32)
-    mean_square = jnp.mean(ends * ends, axis=1, keepdims=True)
-    ends = (ends * lax.rsqrt(mean_square + epsilon) * closing_gain).astype(BF)
-    logits = dot(ends, vocabulary_weight)
-    return done.T, logits
+    logits = head(spread.reshape(columns, groups, 16, 256), closing_gain[None, :], vocabulary_weight.T)
+    return done.T, logits.T
 
 
 def solution(mesh):

time: 306 us -> 322 us (1.052)
  Pallas kernels: 265 us -> 289 us
  matrix products: 14.7 us -> 10.2 us
    pallas_call x1, Pallas kernels: 202 us -> 229 us  [experts_call(): pl.pallas_call(functools.partial(expert_kernel, slots), out_shape=(jax.Sh...]
    pallas_call x1, Pallas kernels: 39 us -> 29.1 us  [out_project(): pl.pallas_call(out_kernel, out_shape=(jax.ShapeDtypeStruct((q, rows), BF)...]
    pallas_call x0 -> x1, Pallas kernels: none -> 6.82 us  [head(): pl.pallas_call(head_kernel, out_shape=jax.ShapeDtypeStruct((entries, spre...]
    dot_general x1 -> x0, matrix products: 4.54 us -> none  [dot(): return jnp.dot(a, b, preferred_element_type=F32)]
    unnamed x35 -> x39, local copies, waits for them, and re-layouts: 8.72 us -> 12.3 us
where the time goes in v4:
time: 322 us; the launch traced here: 321 us
  Pallas kernels  289 us (90%)
  local copies, waits for them, and re-layouts  15.8 us (5%)
  matrix products  10.2 us (3%)
  other arithmetic  5.56 us (2%)
    pallas_call x1, Pallas kernels, experts_call(): pl.pallas_call(functools.partial(expert_kernel, slots), out_shape=(jax.Sh...  229 us
    pallas_call x1, Pallas kernels, out_project(): pl.pallas_call(out_kernel, out_shape=(jax.ShapeDtypeStruct((q, rows), BF)...  29.1 us
    pallas_call x1, Pallas kernels, gather_z(): pl.pallas_call(gather_kernel, out_shape=(jax.ShapeDtypeStruct((n,) + hidd...  23.6 us
    unnamed x39, local copies, waits for them, and re-layouts  12.3 us
    pallas_call x1, Pallas kernels, head(): pl.pallas_call(head_kernel, out_shape=jax.ShapeDtypeStruct((entries, spre...  6.82 us

profile of v4, /device:TPU:1, one launch (start us, length us, event | category | flops | bytes accessed | tf_op | source)
XLA Modules:
  0.0 320.9 jit_solution(16113929377018145085)
XLA Ops:
  0.6 0.8 reduce.1
  1.5 0.8 mul.117
  2.3 0.7 convert_bitcast_fusion.1
  3.0 0.7 fusion.31.a_ref
  3.7 1.0 copy-done.2
  4.8 23.6 %shard_map.194 = (bf16[4,720,384]{2,1,0:T(8,128)(2,1)S(1)}, bf16[4,16,128]{2,1,0:T(8,128)(2,1)S(1)}) custom-call(bf16[720,384]{1,0:T(8,128)(2,1)S(1)} %bitcast.62, bf16[16,128]{1,0:T(8,128)(2,1)S(1)} %fusion.31.a_ref), custom_call_target="tpu_custom_call" | custom-call | tf_op jit(solution)/shard_map/pallas_call | solution.py:110
  28.4 0.6 multiply_reduce_fusion
  29.0 0.6 multiply_convert_fusion
  29.6 3.0 fusion.3
  32.6 0.6 fusion.1
  33.3 0.1 select_reduce_fusion
  33.5 3.1 fusion.7
  36.6 1.5 copy.32
  38.2 0.3 multiply_cosine_fusion
  38.6 1.1 fusion.2
  39.8 3.0 fusion.8
  42.9 0.8 dynamic_slice.3
  43.6 0.2 broadcast_in_dim.106.gain_ref
  44.0 1.0 copy-done.9
  45.0 0.9 copy-done.10
  45.9 0.9 copy-done.11
  46.9 29.1 %shard_map.195 = (bf16[720,384]{1,0:T(8,128)(2,1)S(1)}, bf16[720,384]{1,0:T(8,128)(2,1)S(1)}, bf16[2048,384]{1,0:T(8,128)(2,1)S(1)}, bf16[2048,384]{1,0:T(8,128)(2,1)S(1)}) custom-call(bf16[512,384]{1,0:T(8,128)(2,1)S(1)} %bitcast.65, bf16[2880,512]{1,0:T(8,128)(2,1)} %bitcast.71, bf16[512,128]{1,0:T(8,128)(2,1)S(1)} %copy-done.11, ...), custom_call_target="tpu_custom_call" | custom-call | tf_op jit(solution)/shard_map/pallas_call | solution.py:231
  75.9 1.1 copy-done.4
  77.1 1.1 copy-done.5
  78.2 0.8 copy-done.7
  79.0 0.8 copy-done.8
  80.0 0.7 maximum_maximum_fusion.e_ref
  80.7 229.0 %shard_map.196 = (bf16[720,384]{1,0:T(8,128)(2,1)}, bf16[2,16,4,16,256]{4,3,2,1,0:T(8,128)(2,1)}) custom-call(bf16[2048,384]{1,0:T(8,128)(2,1)} %copy-done.4, bf16[2048,384]{1,0:T(8,128)(2,1)} %copy-done.5, bf16[16,384]{1,0:T(8,128)(2,1)} %maximum_maximum_fusion.e_ref, bf16[720,384]{1,0:T(8,128)(2,1)} %copy-done.8, bf16[720,384]{1,0:T(8,128)(2,1)} %copy-done.7, ...), custom_call_target="tpu_custom_call" | custom-call | tf_op jit(solution)/shard_map/pallas_call | solution.py:563
  309.7 2.3 copy-done.1
  312.1 1.2 copy-done.6
  313.3 6.8 %shard_map.197 = f32[800,128]{1,0:T(8,128)} custom-call(bf16[32,4,16,256]{3,2,1,0:T(8,128)(2,1)S(1)} %bitcast.64, f32[1,2880]{1,0:T(1,128)S(1)} %broadcast_in_dim.105.gain_ref, bf16[800,2880]{1,0:T(8,128)(2,1)S(1)} %bitcast.61), custom_call_target="tpu_custom_call" | custom-call | tf_op jit(solution)/shard_map/pallas_call | solution.py:626
  320.1 0.8 copy.42
  (47 shorter events, 1.1 us)
Async XLA Ops:
  0.6 32.8 %copy-start = (bf16[2880,128]{1,0:T(8,128)(2,1)S(1)}, bf16[2880,128]{1,0:T(8,128)(2,1)}, u32[]{:S(2)}) copy-start(bf16[2880,128]{1,0:T(8,128)(2,1)} %param.28) | copy-start | bytes 2211844
  3.7 1.1 copy-start.2
  4.8 24.8 %copy-start.17 = (bf16[2880,1,640]{2,0,1:T(8,128)(2,1)S(1)}, bf16[2880,1,640]{2,0,1:T(8,128)(2,1)}, u32[]{:S(2)}) copy-start(bf16[2880,1,640]{2,0,1:T(8,128)(2,1)} %param.25) | copy-start | bytes 11059204
  29.5 3.0 copy-start.14
  32.6 0.7 copy-start.16
  32.6 0.9 copy-start.13
  38.1 1.6 copy-start.18
  39.8 4.2 %copy-start.3 = (bf16[384,720]{0,1:T(8,128)(2,1)S(1)}, bf16[384,720]{0,1:T(8,128)(2,1)}, u32[]{:S(2)}) copy-start(bf16[384,720]{0,1:T(8,128)(2,1)} %param.19) | copy-start | bytes 1658884
  44.0 1.0 copy-start.9
  45.0 0.9 copy-start.10
  45.9 0.9 copy-start.11
  75.9 1.2 copy-start.4
  77.1 1.1 copy-start.5
  78.2 0.8 copy-start.7
  79.0 0.8 copy-start.8
  80.7 229.0 %copy-start.15 = (f32[2880]{0:T(1024)S(1)}, f32[2880]{0:T(1024)}, u32[]{:S(2)}) copy-start(f32[2880]{0:T(1024)} %param.36) | copy-start | bytes 34564
  309.7 2.3 copy-start.1
  312.1 1.2 copy-start.6
  313.3 6.8 %copy-start.12 = (bf16[720,384]{1,0:T(8,128)(2,1)S(1)}, bf16[720,384]{1,0:T(8,128)(2,1)}, u32[]{:S(2)}) copy-start(bf16[720,384]{1,0:T(8,128)(2,1)} %get-tuple-element.16) | copy-start | bytes 1658884

commit v5 on v4

--- a/solution.py
+++ b/solution.py
@@ -17,7 +17,7 @@
 PER = 4
 EARLY = 3
 AHEAD = 2
-NEXT = 2
+NEXT = 1
 BACK = 1
 ABSORB = 2
 SENDING = 4
@@ -268,18 +268,12 @@
 
 
 def expert_kernel(
-    slots, d_hbm, g_hbm, e_ref, mi_hbm, resid_hbm, wg_hbm, wu_hbm, wd_hbm,
+    slots, d_ref, g_ref, e_ref, mi_ref, resid_ref, wg_hbm, wu_hbm, wd_hbm,
     out_ref, spread_ref,
-    d_ref, g_ref, mi_ref, resid_ref, fetched, mi_nb, stg, xb, wg, wu, wd, raw, yo, ys, yr, ans, macc, m1s, m1r, e1s, e1r, pk,
+    mi_nb, stg, xb, wg, wu, wd, raw, yo, ys, yr, ans, macc, m1s, m1r, e1s, e1r, pk,
     w_sem, mi_sem, ds, dr, zs, zr, ps, pr, bs, br, own_sem, m_sem, ks, kr, ss, sr,
 ):
     z, n, c, m = place()
-    loads = [
-        pltpu.make_async_copy(src, dst, fetched.at[i])
-        for i, (src, dst) in enumerate(((mi_hbm, mi_ref), (d_hbm, d_ref), (g_hbm, g_ref), (resid_hbm, resid_ref)))
-    ]
-    for load in loads:
-        load.start()
     span = PER * slots
     q = mi_ref.shape[0]
 
@@ -304,7 +298,6 @@
     for o in (1, 2, 3):
         pl.semaphore_signal(barrier, inc=1, device_id=(lax.rem(z + o, n), c), device_id_type=MESH)
     pl.semaphore_wait(barrier, m + 2)
-    loads[0].wait()
     first = send(mi_ref, mi_nb, mi_sem.at[0], mi_sem.at[1], (near(0), c))
 
     def block(j):
@@ -417,7 +410,6 @@
 
     fetch(0).start()
 
-    loads[1].wait()
     head = 2
 
     @pl.loop(0, head)
@@ -425,8 +417,6 @@
         dispatch(ch, 0)
 
     macc[...] = jnp.zeros_like(macc)
-    loads[2].wait()
-    loads[3].wait()
     first.wait_recv()
 
     @pl.loop(0, head)
@@ -566,11 +556,9 @@
             jax.ShapeDtypeStruct((q, tokens), BF),
             jax.ShapeDtypeStruct((2, columns // 2, groups, 16, 256), BF),
         ),
-        in_specs=[ANY, ANY, VMEM] + [ANY] * 5,
+        in_specs=[VMEM] * 5 + [ANY] * 3,
         out_specs=(VMEM, ANY),
         scratch_shapes=[
-            pltpu.VMEM(pick.shape, BF), pltpu.VMEM(weigh.shape, BF),
-            pltpu.VMEM((q, tokens), BF), pltpu.VMEM((q, tokens), BF), dma(4),
             pltpu.VMEM((q, tokens), BF),
             sending, big(4),
             pltpu.VMEM((groups * q, f), BF), pltpu.VMEM((groups * q, f), BF), pltpu.VMEM((groups, f, q), BF),

time: 322 us -> 296 us (0.919)
  Pallas kernels: 289 us -> 263 us
    pallas_call x1, Pallas kernels: 229 us -> 203 us  [experts_call(): pl.pallas_call(functools.partial(expert_kernel, slots), out_shape=(jax.Sh...]
where the time goes in v5:
time: 296 us; the launch traced here: 295 us
  Pallas kernels  263 us (89%)
  local copies, waits for them, and re-layouts  15.8 us (5%)
  matrix products  10.2 us (3%)
  other arithmetic  5.56 us (2%)
    pallas_call x1, Pallas kernels, experts_call(): pl.pallas_call(functools.partial(expert_kernel, slots), out_shape=(jax.Sh...  203 us
    pallas_call x1, Pallas kernels, out_project(): pl.pallas_call(out_kernel, out_shape=(jax.ShapeDtypeStruct((q, rows), BF)...  29.1 us
    pallas_call x1, Pallas kernels, gather_z(): pl.pallas_call(gather_kernel, out_shape=(jax.ShapeDtypeStruct((n,) + hidd...  23.6 us
    unnamed x39, local copies, waits for them, and re-layouts  12.3 us
    pallas_call x1, Pallas kernels, head(): pl.pallas_call(head_kernel, out_shape=jax.ShapeDtypeStruct((entries, spre...  6.82 us
    dot_general x2, matrix products, dot_tn(): lax.dot_general(a, b, (((0,), (0,)), ((), ())), preferred_element_type=F32)  6.12 us

profile of v5, /device:TPU:1, one launch (start us, length us, event | category | flops | bytes accessed | tf_op | source)
XLA Modules:
  0.0 295.3 jit_solution(1807577888109983085)
XLA Ops:
  0.6 0.8 reduce.1
  1.5 0.8 mul.117
  2.3 0.7 convert_bitcast_fusion.1
  3.0 0.7 fusion.31.a_ref
  3.7 1.0 copy-done.2
  4.8 23.6 %shard_map.194 = (bf16[4,720,384]{2,1,0:T(8,128)(2,1)S(1)}, bf16[4,16,128]{2,1,0:T(8,128)(2,1)S(1)}) custom-call(bf16[720,384]{1,0:T(8,128)(2,1)S(1)} %bitcast.62, bf16[16,128]{1,0:T(8,128)(2,1)S(1)} %fusion.31.a_ref), custom_call_target="tpu_custom_call" | custom-call | tf_op jit(solution)/shard_map/pallas_call | solution.py:110
  28.4 0.6 multiply_reduce_fusion
  29.0 0.6 multiply_convert_fusion
  29.6 3.0 %fusion.3 = f32[384,640]{1,0:T(8,128)} fusion(bf16[2880,384]{1,0:T(8,128)(2,1)S(1)} %bitcast.72, bf16[2880,1,640]{2,0,1:T(8,128)(2,1)S(1)} %copy-done.17), kind=kOutput, calls=%fused_computation.8 | convolution fusion | flops 1415577600 | bytes 6881280 | tf_op jit(solution)/shard_map/dot_general | solution.py:47
  32.6 0.6 fusion.1
  33.3 0.1 select_reduce_fusion
  33.5 3.1 %fusion.7 = f32[640,384]{0,1:T(8,128)} fusion(f32[384,640]{1,0:T(8,128)} %fusion.3, bf16[2880,384]{1,0:T(8,128)(2,1)S(1)} %fusion.1, bf16[2880,128]{1,0:T(8,128)(2,1)S(1)} %copy-done, bf16[128,1,640]{2,0,1:T(8,128)(2,1)S(1)} %copy-done.13, s32[384]{0:T(512)S(1)} %get-tuple-element.20, s32[128]{0:T(128)S(1)} %and_select_fusion.8), kind=kOutput, calls=%fused_computation.13 | convolution fusion | flops 346669056 | bytes 5081088 | tf_op jit(solution)/shard_map/dot_general | solution.py:47
  36.6 1.5 copy.32
  38.2 0.3 multiply_cosine_fusion
  38.6 1.1 fusion.2
  39.8 3.0 %fusion.8 = bf16[8,384,64]{1,2,0:T(8,128)(2,1)} fusion(f32[8,384,384]{1,2,0:T(8,128)S(1)} %get-tuple-element.26, f32[8,384]{1,0:T(8,128)S(1)} %broadcast_add_fusion, pred[384,384]{0,1:T(8,128)(4,1)S(1)} %fusion.11, f32[640,384]{0,1:T(8,128)} %fusion.7), kind=kOutput, calls=%fused_computation.14 | convolution fusion | flops 155910144 | bytes 5369856 | tf_op jit(solution)/shard_map/hs,gts->ght/dot_general | solution.py:668
  42.9 0.8 dynamic_slice.3
  43.6 0.2 broadcast_in_dim.106.gain_ref
  44.0 1.0 copy-done.9
  45.0 0.9 copy-done.10
  45.9 0.9 copy-done.11
  46.9 29.1 %shard_map.195 = (bf16[720,384]{1,0:T(8,128)(2,1)S(1)}, bf16[720,384]{1,0:T(8,128)(2,1)S(1)}, bf16[2048,384]{1,0:T(8,128)(2,1)S(1)}, bf16[2048,384]{1,0:T(8,128)(2,1)S(1)}) custom-call(bf16[512,384]{1,0:T(8,128)(2,1)S(1)} %bitcast.65, bf16[2880,512]{1,0:T(8,128)(2,1)} %bitcast.71, bf16[512,128]{1,0:T(8,128)(2,1)S(1)} %copy-done.11, ...), custom_call_target="tpu_custom_call" | custom-call | tf_op jit(solution)/shard_map/pallas_call | solution.py:231
  75.9 1.1 copy-done.4
  77.1 1.1 copy-done.5
  78.2 0.8 copy-done.7
  79.0 0.8 copy-done.8
  80.0 0.7 maximum_maximum_fusion.e_ref
  80.7 203.4 %shard_map.196 = (bf16[720,384]{1,0:T(8,128)(2,1)}, bf16[2,16,4,16,256]{4,3,2,1,0:T(8,128)(2,1)}) custom-call(bf16[2048,384]{1,0:T(8,128)(2,1)} %copy-done.4, bf16[2048,384]{1,0:T(8,128)(2,1)} %copy-done.5, bf16[16,384]{1,0:T(8,128)(2,1)} %maximum_maximum_fusion.e_ref, bf16[720,384]{1,0:T(8,128)(2,1)} %copy-done.8, bf16[720,384]{1,0:T(8,128)(2,1)} %copy-done.7, ...), custom_call_target="tpu_custom_call" | custom-call | tf_op jit(solution)/shard_map/pallas_call | solution.py:553
  284.1 2.3 copy-done.1
  286.5 1.2 copy-done.6
  287.7 6.8 %shard_map.197 = f32[800,128]{1,0:T(8,128)} custom-call(bf16[32,4,16,256]{3,2,1,0:T(8,128)(2,1)S(1)} %bitcast.64, f32[1,2880]{1,0:T(1,128)S(1)} %broadcast_in_dim.105.gain_ref, bf16[800,2880]{1,0:T(8,128)(2,1)S(1)} %bitcast.61), custom_call_target="tpu_custom_call" | custom-call | tf_op jit(solution)/shard_map/pallas_call | solution.py:614
  294.5 0.8 copy.42
  (47 shorter events, 1.1 us)
Async XLA Ops:
  0.6 32.8 %copy-start = (bf16[2880,128]{1,0:T(8,128)(2,1)S(1)}, bf16[2880,128]{1,0:T(8,128)(2,1)}, u32[]{:S(2)}) copy-start(bf16[2880,128]{1,0:T(8,128)(2,1)} %param.28) | copy-start | bytes 2211844
  3.7 1.1 copy-start.2
  4.8 24.8 %copy-start.17 = (bf16[2880,1,640]{2,0,1:T(8,128)(2,1)S(1)}, bf16[2880,1,640]{2,0,1:T(8,128)(2,1)}, u32[]{:S(2)}) copy-start(bf16[2880,1,640]{2,0,1:T(8,128)(2,1)} %param.25) | copy-start | bytes 11059204
  29.5 3.0 %copy-start.14 = (f32[2880]{0:T(1024)S(1)}, f32[2880]{0:T(1024)}, u32[]{:S(2)}) copy-start(f32[2880]{0:T(1024)} %param.24) | copy-start | bytes 34564
  32.6 0.7 copy-start.16
  32.6 0.9 copy-start.13
  38.1 1.6 copy-start.18
  39.8 4.2 %copy-start.3 = (bf16[384,720]{0,1:T(8,128)(2,1)S(1)}, bf16[384,720]{0,1:T(8,128)(2,1)}, u32[]{:S(2)}) copy-start(bf16[384,720]{0,1:T(8,128)(2,1)} %param.19) | copy-start | bytes 1658884
  44.0 1.0 copy-start.9
  45.0 0.9 copy-start.10
  45.9 0.9 copy-start.11
  75.9 1.2 copy-start.4
  77.1 1.1 copy-start.5
  78.2 0.8 copy-start.7
  79.0 0.8 copy-start.8
  80.7 203.4 %copy-start.15 = (f32[2880]{0:T(1024)S(1)}, f32[2880]{0:T(1024)}, u32[]{:S(2)}) copy-start(f32[2880]{0:T(1024)} %param.36) | copy-start | bytes 34564
  284.1 2.3 copy-start.1
  286.5 1.2 copy-start.6
  287.7 6.8 %copy-start.12 = (bf16[720,384]{1,0:T(8,128)(2,1)S(1)}, bf16[720,384]{1,0:T(8,128)(2,1)}, u32[]{:S(2)}) copy-start(bf16[720,384]{1,0:T(8,128)(2,1)} %get-tuple-element.16) | copy-start | bytes 1658884
